TPU v7x, 512 devices: a whole 4x4x16 slice. The times are simulated.
512 devices in a mesh: orient: 32 (over y_lo, z), brow: 2 (over core), bcol: 8 (over x, y_hi).
Axes of the slice: x: 4, y: 4 (y_hi: 2, y_lo: 2; y = y_hi * 2 + y_lo), z: 16, core: 2. Of those that a mesh axis runs over, the one named last changes fastest.
Arguments:
- volume: float32 [32, 64, 832], P('orient', 'brow', 'bcol'), may hold values from -700 to 700
- template: float32 [24, 24, 24], replicated, may hold values from 0 to 1
- voxel_maps: int32 [32, 13824], P('orient'), may hold values from 0 to 13823, as said below
Outputs:
- best: float32 [32, 64, 832], P('orient', 'brow', 'bcol')
Inputs may be any that keep to these rules, and one draw needn't show every extreme that they name: `voxel_maps`: each row holds every number of 0 to 13823 exactly once.
All inputs are finite; a program needn't handle non-finite values.
Results may differ from a plain program's by a relative error of at most 0.00013.
Values sent between devices are 32-bit elements; how exact they have to be, the bound alone decides.
No kernel may reach another device: no remote copies, remote signals or barrier semaphores. Data moves between devices by JAX's collectives and lax.ppermute only.
A program may use at most 64 MiB of HBM per device.

v0:
```python
import math

import jax
import jax.numpy as jnp
from jax import lax
from jax.sharding import PartitionSpec as P

epsilon = 1e-06
floor_share = 0.1
highest = lax.Precision.HIGHEST


def extended(cells, sides, width):
    for axis, dim in sides:
        count = lax.axis_size(axis)
        ends = count - 1
        head = lax.slice_in_dim(cells, 0, width, axis=dim)
        tail = lax.slice_in_dim(cells, cells.shape[dim] - width, cells.shape[dim], axis=dim)
        cells = jnp.concatenate(
            [
                lax.ppermute(tail, axis, [(i, (i + 1) % count) for i in range(ends)]),
                cells,
                lax.ppermute(head, axis, [((i + 1) % count, i) for i in range(ends)]),
            ],
            axis=dim,
        )
    return cells


def phase_tables(row_index, col_index, length):
    products = row_index[:, None] * col_index[None, :] % length
    angles = products.astype(jnp.float32) * (2.0 * math.pi / length)
    return (jnp.cos(angles), jnp.sin(angles))


def band_table(row_index, col_index, lower, upper):
    offsets = col_index[None, :] - row_index[:, None]
    return ((offsets >= lower) & (offsets < upper)).astype(jnp.float32)


def whiten_rows(rows_in):
    length = rows_in.shape[-1]
    frequency = jnp.arange(length, dtype=jnp.int32)
    cosine, sine_table = phase_tables(frequency, frequency, length)
    spec_real = jnp.dot(rows_in, cosine, precision=highest)
    spec_imag = -jnp.dot(rows_in, sine_table, precision=highest)
    power_spec = spec_real * spec_real + spec_imag * spec_imag
    smoothed = (
        jnp.roll(power_spec, 1, axis=1) + power_spec + jnp.roll(power_spec, -1, axis=1)
    ) / 3.0
    smoothed = smoothed + floor_share * jnp.mean(power_spec, axis=1, keepdims=True) + epsilon
    weights = lax.rsqrt(smoothed)
    whitened = jnp.dot(spec_real * weights, cosine, precision=highest) - jnp.dot(
        spec_imag * weights, sine_table, precision=highest
    )
    return whitened / math.sqrt(length)


def shards(volume, template, voxel_maps):
    plane_count, brick_rows, brick_cols = volume.shape
    template_edge = template.shape[0]
    half_edge = template_edge // 2
    depth_total = plane_count * lax.axis_size("orient")
    pad_rows = brick_rows + template_edge
    pad_cols = brick_cols + template_edge
    pad_depth = depth_total + template_edge
    pencils = lax.all_to_all(volume, "bcol", split_axis=1, concat_axis=2, tiled=True)
    whitened_rows = whiten_rows(pencils.reshape(-1, pencils.shape[-1])).reshape(pencils.shape)
    whitened = lax.all_to_all(whitened_rows, "bcol", split_axis=2, concat_axis=1, tiled=True)
    padded = extended(whitened, (("brow", 1), ("bcol", 2)), half_edge)
    col_freq = jnp.arange(pad_cols, dtype=jnp.int32)
    row_freq = jnp.arange(pad_rows, dtype=jnp.int32)
    depth_freq = jnp.arange(pad_depth, dtype=jnp.int32)
    depth_index = jnp.arange(depth_total, dtype=jnp.int32)
    tpl_index = jnp.arange(template_edge, dtype=jnp.int32)
    out_rows = jnp.arange(brick_rows, dtype=jnp.int32)
    out_cols = jnp.arange(brick_cols, dtype=jnp.int32)
    cos_cols, sin_cols = phase_tables(col_freq, col_freq, pad_cols)
    cos_rows, sin_rows = phase_tables(row_freq, row_freq, pad_rows)
    cos_depth, sin_depth = phase_tables(depth_freq, depth_index, pad_depth)
    tcos_cols, tsin_cols = phase_tables(tpl_index, col_freq, pad_cols)
    tcos_rows, tsin_rows = phase_tables(row_freq, tpl_index, pad_rows)
    tcos_depth, tsin_depth = phase_tables(depth_freq, tpl_index, pad_depth)
    back_depth_c, back_depth_s = phase_tables(depth_index - half_edge, depth_freq, pad_depth)
    back_rows_c, back_rows_s = phase_tables(out_rows, row_freq, pad_rows)
    back_cols_c, back_cols_s = phase_tables(col_freq, out_cols, pad_cols)
    box_rows = band_table(out_rows, row_freq, 0, template_edge)
    box_cols = band_table(out_cols, col_freq, 0, template_edge).T
    box_depth = band_table(depth_index, depth_index, -half_edge, half_edge)
    portion = lax.all_gather(padded, "orient", axis=0, tiled=True)
    col_real = jnp.einsum("nxy,yk->nxk", portion, cos_cols, precision=highest)
    col_imag = -jnp.einsum("nxy,yk->nxk", portion, sin_cols, precision=highest)
    spec_real = jnp.einsum("kx,nxy->nky", cos_rows, col_real, precision=highest) + jnp.einsum(
        "kx,nxy->nky", sin_rows, col_imag, precision=highest
    )
    spec_imag = jnp.einsum("kx,nxy->nky", cos_rows, col_imag, precision=highest) - jnp.einsum(
        "kx,nxy->nky", sin_rows, col_real, precision=highest
    )
    squares = portion * portion
    along_cols = jnp.einsum("nxy,yr->nxr", squares, box_cols, precision=highest)
    sum_real = jnp.einsum("kz,zxy->kxy", cos_depth, spec_real, precision=highest) + jnp.einsum(
        "kz,zxy->kxy", sin_depth, spec_imag, precision=highest
    )
    sum_imag = jnp.einsum("kz,zxy->kxy", cos_depth, spec_imag, precision=highest) - jnp.einsum(
        "kz,zxy->kxy", sin_depth, spec_real, precision=highest
    )
    sum_energy = jnp.einsum(
        "wz,zqr->wqr",
        box_depth,
        jnp.einsum("qx,nxr->nqr", box_rows, along_cols, precision=highest),
        precision=highest,
    )
    flattened = template.reshape(-1)
    centred = flattened - jnp.mean(flattened)
    normed = centred / jnp.sqrt(jnp.sum(centred * centred) + epsilon)
    voxel_total = flattened.shape[0]
    scaling = lax.rsqrt(sum_energy / voxel_total + epsilon)
    inverse_norm = 1.0 / (pad_depth * pad_rows * pad_cols)
    rotated = normed[voxel_maps[0]].reshape(template_edge, template_edge, template_edge)
    tcol_real = jnp.einsum("abc,ck->abk", rotated, tcos_cols, precision=highest)
    tcol_imag = -jnp.einsum("abc,ck->abk", rotated, tsin_cols, precision=highest)
    trow_real = jnp.einsum("kb,abc->akc", tcos_rows, tcol_real, precision=highest) + jnp.einsum(
        "kb,abc->akc", tsin_rows, tcol_imag, precision=highest
    )
    trow_imag = jnp.einsum("kb,abc->akc", tcos_rows, tcol_imag, precision=highest) - jnp.einsum(
        "kb,abc->akc", tsin_rows, tcol_real, precision=highest
    )
    tpl_real = jnp.einsum("ka,abc->kbc", tcos_depth, trow_real, precision=highest) + jnp.einsum(
        "ka,abc->kbc", tsin_depth, trow_imag, precision=highest
    )
    tpl_imag = jnp.einsum("ka,abc->kbc", tcos_depth, trow_imag, precision=highest) - jnp.einsum(
        "ka,abc->kbc", tsin_depth, trow_real, precision=highest
    )
    prod_real = sum_real * tpl_real + sum_imag * tpl_imag
    prod_imag = sum_imag * tpl_real - sum_real * tpl_imag
    depth_real = jnp.einsum("zk,kxy->zxy", back_depth_c, prod_real, precision=highest) - jnp.einsum(
        "zk,kxy->zxy", back_depth_s, prod_imag, precision=highest
    )
    depth_imag = jnp.einsum("zk,kxy->zxy", back_depth_c, prod_imag, precision=highest) + jnp.einsum(
        "zk,kxy->zxy", back_depth_s, prod_real, precision=highest
    )
    rows_real = jnp.einsum("qk,zky->zqy", back_rows_c, depth_real, precision=highest) - jnp.einsum(
        "qk,zky->zqy", back_rows_s, depth_imag, precision=highest
    )
    rows_imag = jnp.einsum("qk,zky->zqy", back_rows_c, depth_imag, precision=highest) + jnp.einsum(
        "qk,zky->zqy", back_rows_s, depth_real, precision=highest
    )
    correlation = jnp.einsum("zqk,kr->zqr", rows_real, back_cols_c, precision=highest) - jnp.einsum(
        "zqk,kr->zqr", rows_imag, back_cols_s, precision=highest
    )
    score = correlation * inverse_norm * scaling
    combined = lax.pmax(score, "orient")
    return lax.dynamic_slice_in_dim(
        combined, lax.axis_index("orient") * plane_count, plane_count, 0
    )


def solution(mesh):
    in_specs = (P("orient", "brow", "bcol"), P(), P("orient", None))
    out_specs = P("orient", "brow", "bcol")
    return jax.shard_map(shards, mesh=mesh, in_specs=in_specs, out_specs=out_specs, check_vma=False)
```

profile of v0, /device:TPU:6, one launch (start us, length us, event | category | flops | bytes accessed | tf_op | source)
XLA Modules:
  0.0 549.7 jit_solution(6854731164237918820)
XLA Ops:
  6.5 9.3 %all-to-all-start = ((f32[1,32,104]{2,0,1:T(1,128)}), f32[1,32,104]{2,0,1:T(1,128)S(1)}, u32[]{:S(2)}, u32[]{:S(2)}) async-start(f32[1,32,104]{2,0,1:T(1,128)} %bitcast.154), calls=%async_computation | async-start | bytes 32768 | tf_op jit(solution)/shard_map/all_to_all | solution.py:67
  15.8 1.6 reduce_sum.28
  18.1 1.6 multiply_reduce_fusion
  21.8 71.2 %gather_fusion = f32[13824]{0:T(1024)S(1)} fusion(f32[13824]{0:T(1024)S(1)} %div.38, s32[14336]{0:T(1024)S(1)} %pad_clamp_fusion), kind=kCustom, calls=%fused_computation | custom fusion | bytes 165888 | tf_op jit(solution)/shard_map/gather | solution.py:119
  101.4 13.9 %fusion.35 = f32[4,832]{1,0:T(4,128)S(1)} fusion(f32[4,832]{1,0:T(4,128)S(1)} %reshape.51), kind=kOutput, calls=%fused_computation.48 | convolution fusion | flops 39456768 | bytes 26624 | tf_op jit(solution)/shard_map/dot_general | solution.py:45
  115.3 14.1 %fusion.421 = (f32[4]{0:T(128)S(1)}, f32[4,832]{1,0:T(4,128)S(1)}, f32[832,4]{0,1:T(4,128)S(1)}) fusion(f32[4,832]{1,0:T(4,128)S(1)} %fusion.35, f32[4,832]{1,0:T(4,128)S(1)} %reshape.51), kind=kOutput, calls=%fused_computation.402 | convolution fusion | flops 39470076 | bytes 53264 | tf_op jit(solution)/shard_map/dot_general | solution.py:46
  129.7 14.1 %fusion.6 = f32[4,832]{1,0:T(4,128)S(1)} fusion(f32[4,832]{1,0:T(4,128)S(1)} %fusion.35, f32[4,832]{1,0:T(4,128)S(1)} %fusion.186), kind=kOutput, calls=%fused_computation.9 | convolution fusion | flops 39460096 | bytes 39936 | tf_op jit(solution)/shard_map/dot_general | solution.py:53
  143.8 13.7 %fusion.44 = f32[1,4,832]{2,1,0:T(4,128)S(1)} fusion(f32[4,832]{1,0:T(4,128)S(1)} %fusion.6, f32[4,832]{1,0:T(4,128)S(1)} %fusion.186, f32[832,4]{0,1:T(4,128)S(1)} %get-tuple-element.17), kind=kOutput, calls=%fused_computation.51 | convolution fusion | flops 39470080 | bytes 53248 | tf_op jit(solution)/shard_map/dot_general | solution.py:53
  158.7 1.7 reduce.4
  161.3 7.2 %all-to-all-start.1 = ((f32[8,1,416]{2,1,0:T(1,128)}), f32[8,1,416]{2,1,0:T(1,128)S(1)}, u32[]{:S(2)}, u32[]{:S(2)}) async-start(f32[8,1,416]{2,1,0:T(1,128)} %reshape.82), calls=%async_computation.1 | async-start | bytes 32768 | tf_op jit(solution)/shard_map/all_to_all | solution.py:69
  168.5 2.6 fusion.65
  171.1 3.0 all-to-all-done.1
  178.7 3.0 collective-permute-start
  181.7 2.7 convolution_add_fusion.1
  184.5 2.5 collective-permute-start.3
  187.0 4.8 collective-permute-start.2
  191.9 3.3 collective-permute-done.2
  195.3 71.5 %all_gather.3 = f32[32,56,128]{2,1,0:T(8,128)S(1)} all-gather(f32[1,56,128]{2,1,0:T(8,128)S(1)} %pad_maximum_fusion.1), channel_id=1, replica_groups=mesh['orient'=32,'brow'=2,'bcol'=8] {'orient'}, dimensions={0}, use_global_device_ids=true | all-gather | bytes 946176 | tf_op jit(solution)/shard_map/all_gather | solution.py:90
  272.7 1.5 fusion.55
  275.4 1.5 fusion.59
  276.9 1.5 convolution_subtract_fusion
  278.5 2.3 multiply_subtract_fusion
  292.1 1.8 fusion.34
  294.0 247.2 %all-reduce.2.cloned.1.call-done = f32[32,32,104]{2,1,0:T(8,128)} async-done(((f32[32,32,104]{2,1,0:T(8,128)}), f32[32,32,104]{2,1,0:T(8,128)}) %all-reduce.2.cloned.1.call-update) | async-done | bytes 426000 | tf_op jit(solution)/shard_map/pmax | solution.py:152
  (62 shorter events, 36.3 us)
Async XLA Ops:
  6.5 15.1 %copy-start.2 = (s32[1,13824]{1,0:T(1,128)S(1)}, s32[1,13824]{1,0:T(1,128)}, u32[]{:S(2)}) copy-start(s32[1,13824]{1,0:T(1,128)} %param.5) | copy-start | bytes 165892
  6.5 94.8 %all-to-all-start = ((f32[1,32,104]{2,0,1:T(1,128)}), f32[1,32,104]{2,0,1:T(1,128)S(1)}, u32[]{:S(2)}, u32[]{:S(2)}) async-start(f32[1,32,104]{2,0,1:T(1,128)} %bitcast.154), calls=%async_computation | async-start | bytes 32768 | tf_op jit(solution)/shard_map/all_to_all | solution.py:67
  96.5 1.5 copy-start
  98.9 0.9 copy-start.1
  161.3 12.8 %all-to-all-start.1 = ((f32[8,1,416]{2,1,0:T(1,128)}), f32[8,1,416]{2,1,0:T(1,128)S(1)}, u32[]{:S(2)}, u32[]{:S(2)}) async-start(f32[8,1,416]{2,1,0:T(1,128)} %reshape.82), calls=%async_computation.1 | async-start | bytes 32768 | tf_op jit(solution)/shard_map/all_to_all | solution.py:69
  168.5 372.7 %all-reduce.2.cloned.1.call-start = ((), (), s32[]{:S(2)}) async-start(), calls=%async_computation.2 | async-start | bytes 1048576 | tf_op jit(solution)/shard_map/pmax | solution.py:152
  177.4 7.0 %collective-permute-start.1 = (f32[1,12,104]{2,1,0:T(8,128)S(1)}, f32[1,12,104]{2,1,0:T(8,128)S(1)}, u32[]{:S(2)}, u32[]{:S(2)}) collective-permute-start(f32[1,12,104]{2,1,0:T(8,128)S(1)} %get-tuple-element.12), channel_id=1, source_target_pairs={{8,0},{9,1},{10,2},{11,3},{12,4},{13,5},{14,6},{15,7},{24,16},{25,... | collective-permute-start | bytes 14984 | tf_op jit(solution)/shard_map/ppermute | solution.py:23
  178.7 5.7 %collective-permute-start = (f32[1,12,104]{2,1,0:T(8,128)S(1)}, f32[1,12,104]{2,1,0:T(8,128)S(1)}, u32[]{:S(2)}, u32[]{:S(2)}) collective-permute-start(f32[1,12,104]{2,1,0:T(8,128)S(1)} %get-tuple-element.11), channel_id=1, source_target_pairs={{0,8},{1,9},{2,10},{3,11},{4,12},{5,13},{6,14},{7,15},{16,24},{17,... | collective-permute-start | bytes 14984 | tf_op jit(solution)/shard_map/ppermute | solution.py:21
  184.5 7.4 %collective-permute-start.3 = (f32[1,56,12]{2,1,0:T(8,128)S(1)}, f32[1,56,12]{2,1,0:T(8,128)S(1)}, u32[]{:S(2)}, u32[]{:S(2)}) collective-permute-start(f32[1,56,12]{2,1,0:T(8,128)S(1)} %get-tuple-element.10), channel_id=1, source_target_pairs={{1,0},{2,1},{3,2},{4,3},{5,4},{6,5},{7,6},{9,8},{10,9},{11,10},{12... | collective-permute-start | bytes 8072 | tf_op jit(solution)/shard_map/ppermute | solution.py:23
  187.0 8.2 %collective-permute-start.2 = (f32[1,56,12]{2,1,0:T(8,128)S(1)}, f32[1,56,12]{2,1,0:T(8,128)S(1)}, u32[]{:S(2)}, u32[]{:S(2)}) collective-permute-start(f32[1,56,12]{2,1,0:T(8,128)S(1)} %get-tuple-element.9), channel_id=1, source_target_pairs={{0,1},{1,2},{2,3},{3,4},{4,5},{5,6},{6,7},{8,9},{9,10},{10,11},{11... | collective-permute-start | bytes 8072 | tf_op jit(solution)/shard_map/ppermute | solution.py:21
Sparse Core Ops, SparseCore 0:
  294.1 247.0 all-reduce.1
where the time goes:
time: 558 us; the launch traced here: 550 us
  waiting for transfers between devices  253 us (45%)
  matrix products  95.3 us (17%)
  local copies, waits for them, and re-layouts  78.7 us (14%)
  blocking collectives  71.5 us (13%)
  starting transfers between devices  28.1 us (5%)
  between operations  15.6 us (3%)
  other arithmetic  7.02 us (1%)
    pmax x1, waiting for transfers between devices, shards(): combined = lax.pmax(score, 'orient')  247 us
    all_gather x1, blocking collectives, shards(): portion = lax.all_gather(padded, 'orient', axis=0, tiled=True)  71.5 us
    gather x1, local copies, waits for them, and re-layouts, shards(): normed[voxel_maps[0]].reshape(template_edge, template_edge, template_edge)  71.2 us
    dot_general x1, matrix products, whiten_rows(): jnp.dot(spec_real * weights, cosine, precision=highest)  14.1 us
    dot_general x1, matrix products, whiten_rows(): spec_imag = -jnp.dot(rows_in, sine_table, precision=highest)  14.1 us
    dot_general x1, matrix products, whiten_rows(): spec_real = jnp.dot(rows_in, cosine, precision=highest)  13.9 us
    dot_general x1, matrix products, whiten_rows(): jnp.dot(spec_imag * weights, sine_table, precision=highest)  13.7 us
  transfers between devices with their start and end apart: 7, of which 3 were waited for; matrix products, arithmetic and copies ran while one was open for 16% of the time, Pallas kernels for 0%

commit v1 on v0

v1 whole, which is shorter than its diff:
```python
import functools
import math

import jax
import jax.numpy as jnp
import ml_dtypes
import numpy as np
from jax import lax
from jax.experimental import pallas as pl
from jax.experimental.pallas import tpu as pltpu
from jax.sharding import Mesh
from jax.sharding import PartitionSpec as P

epsilon = 1e-06
floor_share = 0.1
edge = 24
half = 12
voxels = edge**3
length = 832
cols = 104
window = 128
rows = 32
planes = 32
freqs = length // 2 + 1
freq_pad = 432
group = "ylo", "x", "yhi"
quad_rows = 72
shard_rows = 2 * rows + 2 * quad_rows
blocks = 16
f32 = jnp.float32
bf16 = jnp.bfloat16
nt = (((1,), (1,)), ((), ()))
tn = (((0,), (0,)), ((), ()))


def split_table(table):
    high = table.astype(ml_dtypes.bfloat16)
    low = (table - high.astype(np.float64)).astype(ml_dtypes.bfloat16)
    return high, low


@functools.cache
def dft_tables():
    freq = np.arange(freqs)
    angles = 2.0 * np.pi * ((freq[:, None] * np.arange(length)[None, :]) % length) / length
    forward = np.zeros((2, freq_pad, length))
    forward[0, :freqs] = np.cos(angles)
    forward[1, :freqs] = np.sin(angles)
    counts = np.where((freq == 0) | (freq == freqs - 1), 1.0, 2.0)[:, None] / math.sqrt(length)
    padded = np.zeros((2, freq_pad, length + edge))
    padded[0, :freqs, half : half + length] = np.cos(angles) * counts
    padded[1, :freqs, half : half + length] = np.sin(angles) * counts
    forward = forward.reshape(2 * freq_pad, length)
    padded = padded.reshape(2 * freq_pad, length + edge)
    bricks = length // cols
    backward = np.stack([padded[:, cols * j : cols * j + window] for j in range(bricks)])
    return split_table(forward) + split_table(backward)


def split(values):
    high = values.astype(bf16)
    low = (values - high.astype(f32)).astype(bf16)
    return high, low


def gather_kernel(template_ref, index_ref, out_ref, normed_ref):
    values = template_ref[...]
    centred = values - jnp.sum(values) / voxels
    normed_ref[...] = centred / jnp.sqrt(jnp.sum(centred * centred) + epsilon)
    index = index_ref[...]
    high = index >> 7
    low = index & 127

    def step(row, total):
        table = jnp.broadcast_to(normed_ref[pl.ds(row, 1), :], index.shape)
        found = jnp.take_along_axis(table, low, axis=1, mode="promise_in_bounds")
        return jnp.where(high == row, found, total)

    out_ref[...] = lax.fori_loop(0, voxels // 128, step, jnp.zeros(index.shape, f32))


def whiten_kernel(col_ref, rows_ref, fh_ref, fl_ref, bh_ref, bl_ref, voxels_ref, out_ref, x_ref):
    for plane in range(2):
        for j in range(length // cols):
            x_ref[rows * plane : rows * (plane + 1), cols * j : cols * (j + 1)] = rows_ref[
                plane * 8 + j
            ]
    xh, xl = split(x_ref[...])
    spec = (
        lax.dot_general(fh_ref[...], xh, nt, preferred_element_type=f32)
        + lax.dot_general(fh_ref[...], xl, nt, preferred_element_type=f32)
        + lax.dot_general(fl_ref[...], xh, nt, preferred_element_type=f32)
    )
    real = spec[:freq_pad]
    imag = spec[freq_pad:]
    power = real * real + imag * imag
    k = lax.broadcasted_iota(jnp.int32, power.shape, 0)
    before = jnp.where(k == 0, power[1:2], pltpu.roll(power, 1, 0))
    after = jnp.where(k == freqs - 1, power[freqs - 2 : freqs - 1], pltpu.roll(power, freq_pad - 1, 0))
    total = 2.0 * jnp.sum(power, axis=0, keepdims=True) - power[0:1] - power[freqs - 1 : freqs]
    smoothed = (before + power + after) / 3.0 + floor_share * (total / length) + epsilon
    weights = lax.rsqrt(smoothed)
    wh, wl = split(jnp.concatenate([real * weights, imag * weights], axis=0))
    out_ref[: 2 * rows, :] = (
        lax.dot_general(wh, bh_ref[0], tn, preferred_element_type=f32)
        + lax.dot_general(wl, bh_ref[0], tn, preferred_element_type=f32)
        + lax.dot_general(wh, bl_ref[0], tn, preferred_element_type=f32)
    )
    out_ref[2 * rows :, :] = voxels_ref[...]


def match_kernel(where_ref, g_ref, out_ref, v_ref, l_ref, w_ref, acc_ref, best_ref):
    plane0 = where_ref[0]
    core = where_ref[1]
    first = (core == 0).astype(f32)

    def load_plane(a, energy):
        plane = plane0 - half + a
        valid = jnp.logical_and(plane >= 0, plane < planes).astype(f32)
        plane = jnp.clip(plane, 0, planes - 1)
        z = plane % 16
        start = pl.multiple_of((plane // 16) * rows, rows)
        v_ref[a, half : half + rows, :] = g_ref[core, z, pl.ds(start, rows), :] * valid
        v_ref[a, 0:half, :] = g_ref[0, z, pl.ds(start, rows), :][rows - half :] * (valid * (1.0 - first))
        v_ref[a, half + rows : 56, :] = g_ref[1, z, pl.ds(start, rows), :][:half] * (valid * first)
        full = v_ref[a]
        v_ref[a] = pltpu.roll(full, (a % 4) * 32, 1)
        return energy + full * full

    energy = lax.fori_loop(0, edge, load_plane, jnp.zeros((56, window), f32))

    lane = lax.broadcasted_iota(jnp.int32, (blocks, window), 1)

    def expand(x, carry):
        at = pl.ds(pl.multiple_of(x * blocks, blocks), blocks)
        for quad in range(6):
            total = None
            for part in range(4):
                row = jnp.broadcast_to(v_ref[4 * quad + part, pl.ds(x, 1), :], (blocks, window))
                moved = pltpu.roll(row, 8, 1, stride=8, stride_axis=0)
                total = moved if total is None else jnp.where(lane >= 32 * part, moved, total)
            high, low = split(total)
            l_ref[at, window * quad : window * (quad + 1)] = high
            l_ref[at, 768 + window * quad : 768 + window * (quad + 1)] = low
            l_ref[at, 1536 + window * quad : 1536 + window * (quad + 1)] = high
        return carry

    lax.fori_loop(0, 56, expand, 0)

    def build(b, slot):
        for pair in range(planes // 2):
            for quad in range(6):
                moved = []
                for rot in (2 * pair, 2 * pair + 1):
                    at = 2 * rows + (rot // 16) * quad_rows + quad % 3 + 3 * b
                    row = g_ref[quad // 3, rot % 16, pl.ds(at, 1), :]
                    moved.append(pltpu.roll(jnp.broadcast_to(row, (8, window)), 0, 1, stride=1, stride_axis=0))
                high, low = split(jnp.concatenate(moved, axis=0))
                at = slice(16 * pair, 16 * pair + 16)
                w_ref[slot, at, window * quad : window * (quad + 1)] = high
                w_ref[slot, at, 768 + window * quad : 768 + window * (quad + 1)] = high
                w_ref[slot, at, 1536 + window * quad : 1536 + window * (quad + 1)] = low

    def product(b, slot):
        left = l_ref[pl.ds(pl.multiple_of(b * blocks, blocks), 32 * blocks), :]
        acc_ref[...] += lax.dot_general(left, w_ref[slot], nt, preferred_element_type=f32)

    acc_ref[...] = jnp.zeros_like(acc_ref)
    build(0, 0)

    def step(i, carry):
        build(2 * i + 1, 1)
        product(2 * i, 0)
        build(jnp.minimum(2 * i + 2, edge - 1), 0)
        product(2 * i + 1, 1)
        return carry

    lax.fori_loop(0, edge // 2, step, 0)

    best = jnp.maximum(acc_ref[:, :128], acc_ref[:, 128:])
    for shift in (64, 32, 16, 8):
        best = jnp.maximum(best, pltpu.roll(best, shift, 1))
    best_ref[...] = best
    lanes = lax.broadcasted_iota(jnp.int32, (rows, window), 1)
    score = jnp.zeros((rows, window), f32)
    for block in range(13):
        score = jnp.where(lanes // 8 == block, best_ref[pl.ds(blocks - 1 - block, rows, stride=blocks), :], score)

    def shifted(values, count):
        return pltpu.roll(values, values.shape[0] - count, 0)

    sums = energy
    for count in (1, 2, 4):
        sums = sums + shifted(sums, count)
    sums = sums + shifted(sums, 8) + shifted(sums, 16)
    sums = sums[:rows]
    for count in (1, 2, 4):
        sums = sums + pltpu.roll(sums, window - count, 1)
    sums = sums + pltpu.roll(sums, window - 8, 1) + pltpu.roll(sums, window - 16, 1)
    out_ref[...] = (score * lax.rsqrt(sums / voxels + epsilon))[:, :cols]


def shards(volume, template, voxel_maps):
    ylo, z, core = lax.axis_index("ylo"), lax.axis_index("z"), lax.axis_index("core")
    column = lax.axis_index("x") * 2 + lax.axis_index("yhi")
    vmem = pl.BlockSpec(memory_space=pltpu.VMEM)
    smem = pl.BlockSpec(memory_space=pltpu.SMEM)

    copies = jnp.broadcast_to(volume, (16, rows, cols))
    full_rows = lax.all_to_all(copies, group, split_axis=0, concat_axis=0, tiled=True)

    maps = voxel_maps.reshape(2, half, edge, edge)
    maps = jnp.pad(maps, ((0, 0), (0, 0), (0, 0), (0, 8)), constant_values=-1)
    maps = maps.transpose(0, 2, 1, 3).reshape(2, quad_rows, 128)
    own = lax.dynamic_index_in_dim(maps, core, 0, keepdims=False)
    other = lax.ppermute(own, "ylo", [(0, 1), (1, 0)])
    index = jnp.concatenate([jnp.where(ylo == 0, own, other), jnp.where(ylo == 0, other, own)])
    rotated = pl.pallas_call(
        gather_kernel,
        out_shape=jax.ShapeDtypeStruct((2 * quad_rows, 128), f32),
        in_specs=[vmem, vmem],
        out_specs=vmem,
        scratch_shapes=[pltpu.VMEM((voxels // 128, 128), f32)],
        name="rotate",
    )(template.reshape(voxels // 128, 128), index)

    tables = [jnp.asarray(table) for table in dft_tables()]
    shard = pl.pallas_call(
        whiten_kernel,
        out_shape=jax.ShapeDtypeStruct((shard_rows, 128), f32),
        grid_spec=pltpu.PrefetchScalarGridSpec(
            num_scalar_prefetch=1,
            grid=(1,),
            in_specs=[
                pl.BlockSpec((16, rows, cols), lambda i, c: (0, 0, 0)),
                pl.BlockSpec((2 * freq_pad, length), lambda i, c: (0, 0)),
                pl.BlockSpec((2 * freq_pad, length), lambda i, c: (0, 0)),
                pl.BlockSpec((1, 2 * freq_pad, window), lambda i, c: (c[0], 0, 0)),
                pl.BlockSpec((1, 2 * freq_pad, window), lambda i, c: (c[0], 0, 0)),
                pl.BlockSpec((2 * quad_rows, 128), lambda i, c: (0, 0)),
            ],
            out_specs=pl.BlockSpec((shard_rows, 128), lambda i, c: (0, 0)),
            scratch_shapes=[pltpu.VMEM((2 * rows, length), f32)],
        ),
        compiler_params=pltpu.CompilerParams(vmem_limit_bytes=32 * 2**20),
        name="whiten",
    )(column[None].astype(jnp.int32), full_rows, *tables, rotated)

    gathered = lax.all_gather(shard, "z", axis=0, tiled=True)
    gathered = lax.all_gather(gathered, "core", axis=0, tiled=True)
    place = jnp.stack([ylo * 16 + z, core]).astype(jnp.int32)
    best = pl.pallas_call(
        match_kernel,
        out_shape=jax.ShapeDtypeStruct((rows, cols), f32),
        in_specs=[smem, vmem],
        out_specs=vmem,
        scratch_shapes=[
            pltpu.VMEM((edge, 56, window), f32),
            pltpu.VMEM((56 * blocks, 2304), bf16),
            pltpu.VMEM((2, 256, 2304), bf16),
            pltpu.VMEM((32 * blocks, 256), f32),
            pltpu.VMEM((32 * blocks, 128), f32),
        ],
        compiler_params=pltpu.CompilerParams(vmem_limit_bytes=48 * 2**20),
        name="match",
    )(place, gathered.reshape(2, 16, shard_rows, 128))
    return best[None]


def solution(mesh):
    inner = Mesh(mesh.devices.reshape(2, 16, 2, 4, 2), ("ylo", "z", "core", "x", "yhi"))
    orient, bricks = ("ylo", "z"), ("x", "yhi")
    return jax.shard_map(
        shards,
        mesh=inner,
        in_specs=(P(orient, "core", bricks), P(), P(orient, None)),
        out_specs=P(orient, "core", bricks),
        check_vma=False,
    )
```

time: 558 us -> 190 us (0.34)
  the two profiles are of different devices: /device:TPU:6 before, /device:TPU:1 now
where the time goes in v1:
time: 190 us; the launch traced here: 189 us
  waiting for transfers between devices  101 us (53%)
  Pallas kernels  46.5 us (24%)
  local copies, waits for them, and re-layouts  14.7 us (8%)
  between operations  13.5 us (7%)
  starting transfers between devices  10.6 us (6%)
  other arithmetic  2.46 us (1%)
    all_gather x1, waiting for transfers between devices, shards(): gathered = lax.all_gather(shard, 'z', axis=0, tiled=True)  68.7 us
    all_gather x1, waiting for transfers between devices, shards(): gathered = lax.all_gather(gathered, 'core', axis=0, tiled=True)  32.5 us
    pallas_call x1, Pallas kernels, shards(): pl.pallas_call(match_kernel, out_shape=jax.ShapeDtypeStruct((rows, cols),...  29.4 us
    pallas_call x1, Pallas kernels, shards(): pl.pallas_call(gather_kernel, out_shape=jax.ShapeDtypeStruct((2 * quad_ro...  14.2 us
    all_to_all x1, starting transfers between devices, shards(): lax.all_to_all(copies, group, split_axis=0, concat_axis=0, tiled=True)  6.51 us
    unnamed x16, local copies, waits for them, and re-layouts  6.28 us
    ppermute x1, starting transfers between devices, shards(): other = lax.ppermute(own, 'ylo', [(0, 1), (1, 0)])  4.02 us
  transfers between devices with their start and end apart: 4, of which 2 were waited for; matrix products, arithmetic and copies ran while one was open for 2% of the time, Pallas kernels for 8%

profile of v1, /device:TPU:1, one launch (start us, length us, event | category | flops | bytes accessed | tf_op | source)
XLA Modules:
  0.0 189.0 jit_solution(14485505957489359234)
XLA Ops:
  6.5 1.0 reduce
  7.5 0.9 reshape.13
  8.4 1.2 copy.9
  9.6 0.8 pad_bitcast_fusion
  10.4 1.8 reshape.14
  12.1 1.4 dynamic-slice_bitcast_fusion
  13.5 4.0 %collective-permute-start = (s32[72,128]{1,0:T(8,128)}, s32[72,128]{1,0:T(8,128)}, u32[]{:S(2)}, u32[]{:S(2)}) collective-permute-start(s32[72,128]{1,0:T(8,128)} %dynamic-slice_bitcast_fusion), channel_id=1, source_target_pairs={{0,256},{256,0},{1,257},{257,1},{2,258},{258,2},{3,259},{259,3},{4... | collective-permute-start | bytes 110600 | tf_op jit(solution)/shard_map/ppermute | solution.py:216
  17.5 0.7 broadcast_in_dim.15
  18.3 6.5 %all-to-all-start = ((f32[16,32,104]{2,1,0:T(8,128)}), f32[16,32,104]{2,1,0:T(8,128)}, u32[]{:S(2)}, u32[]{:S(2)}) async-start(f32[16,32,104]{2,1,0:T(8,128)} %broadcast_in_dim.15), calls=%async_computation | async-start | bytes 524288 | tf_op jit(solution)/shard_map/all_to_all | solution.py:210
  24.8 1.8 reshape.12.template_ref
  26.6 0.8 broadcast_select_fusion.1
  27.4 0.6 pad_add_fusion.index_ref
  28.0 14.2 %rotate.1.voxels_ref = f32[144,128]{1,0:T(8,128)} custom-call(f32[108,128]{1,0:T(8,128)} %reshape.12.template_ref, s32[144,128]{1,0:T(8,128)} %pad_add_fusion.index_ref), custom_call_target="tpu_custom_call" | custom-call | tf_op jit(solution)/shard_map/rotate/pallas_call | solution.py:218
  42.2 1.4 copy-done.3
  43.6 1.4 copy-done.4
  45.0 0.9 copy-done.6
  45.9 2.9 %whiten.1 = f32[208,128]{1,0:T(8,128)S(1)} custom-call(s32[1]{0:T(128)} %bitcast.2.col_ref, f32[16,32,104]{2,1,0:T(8,128)} %all-to-all-done.rows_ref, bf16[864,832]{1,0:T(8,128)(2,1)S(1)} %copy-done.4, bf16[864,832]{1,0:T(8,128)(2,1)S(1)} %copy-done.3, bf16[8,864,128]{2,1,0:T(8,128)(2,1)S(1)} %copy-done.2, bf16[8,864,128]{2,1,0:T(8,128)(2,1)S(1)} %copy-done.1, ...), custom_call_target="tpu_custom_call" | custom-call | tf_op jit(solution)/shard_map/whiten/pallas_call | solution.py:228
  48.9 0.6 copy-done.5
  49.5 0.0 all-gather.5.cloned.1.call-start
  49.6 68.7 %all-gather.3.cloned.1.call-done = f32[3328,128]{1,0:T(8,128)} async-done(((f32[208,128]{1,0:T(8,128)}), f32[3328,128]{1,0:T(8,128)}) %all-gather.3.cloned.1.call-update) | async-done | bytes 1703952 | tf_op jit(solution)/shard_map/all_gather | solution.py:249
  118.3 0.1 pad_add_fusion.1.where_ref
  118.4 32.5 %all-gather.5.cloned.1.call-done = f32[6656,128]{1,0:T(8,128)} async-done(((f32[3328,128]{1,0:T(8,128)}), f32[6656,128]{1,0:T(8,128)}) %all-gather.5.cloned.1.call-update) | async-done | bytes 3407888 | tf_op jit(solution)/shard_map/all_gather | solution.py:250
  150.9 2.0 %copy-done = f32[6656,128]{1,0:T(8,128)S(1)} copy-done((f32[6656,128]{1,0:T(8,128)S(1)}, f32[6656,128]{1,0:T(8,128)}, u32[]{:S(2)}) %copy-start) | copy-done | bytes 3407896
  152.8 29.4 %match.1 = f32[32,104]{1,0:T(8,128)} custom-call(s32[2]{0:T(128)S(1)} %pad_add_fusion.1.where_ref, f32[2,16,208,128]{3,2,1,0:T(8,128)S(1)} %bitcast.12), custom_call_target="tpu_custom_call" | custom-call | tf_op jit(solution)/shard_map/match/pallas_call | solution.py:252
  (16 shorter events, 0.1 us)
Async XLA Ops:
  6.5 11.0 %copy-start.7 = (f32[1,32,104]{2,1,0:T(8,128)S(1)}, f32[1,32,104]{2,1,0:T(8,128)}, u32[]{:S(2)}) copy-start(f32[1,32,104]{2,1,0:T(8,128)} %param.7) | copy-start | bytes 39940
  8.4 33.8 %copy-start.1 = (bf16[8,864,128]{2,1,0:T(8,128)(2,1)S(1)}, bf16[8,864,128]{2,1,0:T(8,128)(2,1)}, u32[]{:S(2)}) copy-start(bf16[8,864,128]{2,1,0:T(8,128)(2,1)} %constant.43.clone.bl_ref) | copy-start | bytes 5308420
  8.4 33.8 %copy-start.2 = (bf16[8,864,128]{2,1,0:T(8,128)(2,1)S(1)}, bf16[8,864,128]{2,1,0:T(8,128)(2,1)}, u32[]{:S(2)}) copy-start(bf16[8,864,128]{2,1,0:T(8,128)(2,1)} %constant.42.clone.bh_ref) | copy-start | bytes 5308420
  13.5 13.1 %collective-permute-start = (s32[72,128]{1,0:T(8,128)}, s32[72,128]{1,0:T(8,128)}, u32[]{:S(2)}, u32[]{:S(2)}) collective-permute-start(s32[72,128]{1,0:T(8,128)} %dynamic-slice_bitcast_fusion), channel_id=1, source_target_pairs={{0,256},{256,0},{1,257},{257,1},{2,258},{258,2},{3,259},{259,3},{4... | collective-permute-start | bytes 110600 | tf_op jit(solution)/shard_map/ppermute | solution.py:216
  18.3 24.0 %all-to-all-start = ((f32[16,32,104]{2,1,0:T(8,128)}), f32[16,32,104]{2,1,0:T(8,128)}, u32[]{:S(2)}, u32[]{:S(2)}) async-start(f32[16,32,104]{2,1,0:T(8,128)} %broadcast_in_dim.15), calls=%async_computation | async-start | bytes 524288 | tf_op jit(solution)/shard_map/all_to_all | solution.py:210
  24.8 93.5 %all-gather.3.cloned.1.call-start = ((), (), s32[]{:S(2)}) async-start(), calls=%async_computation.1 | async-start | bytes 1810432 | tf_op jit(solution)/shard_map/all_gather | solution.py:249
  42.2 1.4 copy-start.3
  43.6 1.4 copy-start.4
  45.0 0.9 copy-start.6
  48.9 0.6 copy-start.5
  49.5 101.3 %all-gather.5.cloned.1.call-start = ((), (), s32[]{:S(2)}) async-start(), calls=%async_computation.2 | async-start | bytes 5111808 | tf_op jit(solution)/shard_map/all_gather | solution.py:250
  150.9 2.0 %copy-start = (f32[6656,128]{1,0:T(8,128)S(1)}, f32[6656,128]{1,0:T(8,128)}, u32[]{:S(2)}) copy-start(f32[6656,128]{1,0:T(8,128)} %all-gather.5.cloned.1.call-done) | copy-start | bytes 10223620
Sparse Core Ops, SparseCore 0:
  49.6 68.5 all-gather.2
  120.3 30.4 all-gather.4

commit v2 on v1

v2 whole, which is shorter than its diff:
```python
import functools
import math

import jax
import jax.numpy as jnp
import ml_dtypes
import numpy as np
from jax import lax
from jax.experimental import pallas as pl
from jax.experimental.pallas import tpu as pltpu
from jax.sharding import Mesh
from jax.sharding import PartitionSpec as P

epsilon = 1e-06
floor_share = 0.1
edge = 24
half = 12
voxels = edge**3
length = 832
cols = 104
window = 128
rows = 32
planes = 32
freqs = length // 2 + 1
freq_pad = 432
group = "ylo", "x", "yhi"
half_rows = 60
shard_rows = 2 * rows + half_rows
span = planes // 2 + edge
rots = 16
blocks = 16
depth = 32 * edge
f32 = jnp.float32
bf16 = jnp.bfloat16
nt = (((1,), (1,)), ((), ()))
tn = (((0,), (0,)), ((), ()))


def split_table(table):
    high = table.astype(ml_dtypes.bfloat16)
    low = (table - high.astype(np.float64)).astype(ml_dtypes.bfloat16)
    return high, low


@functools.cache
def dft_tables():
    freq = np.arange(freqs)
    angles = 2.0 * np.pi * ((freq[:, None] * np.arange(length)[None, :]) % length) / length
    forward = np.zeros((2, freq_pad, length))
    forward[0, :freqs] = np.cos(angles)
    forward[1, :freqs] = np.sin(angles)
    counts = np.where((freq == 0) | (freq == freqs - 1), 1.0, 2.0)[:, None] / math.sqrt(length)
    padded = np.zeros((2, freq_pad, length + edge))
    padded[0, :freqs, half : half + length] = np.cos(angles) * counts
    padded[1, :freqs, half : half + length] = np.sin(angles) * counts
    forward = forward.reshape(2 * freq_pad, length)
    padded = padded.reshape(2 * freq_pad, length + edge)
    bricks = length // cols
    backward = np.stack([padded[:, cols * j : cols * j + window] for j in range(bricks)])
    return split_table(forward) + split_table(backward)


def split(values):
    high = values.astype(bf16)
    low = (values - high.astype(f32)).astype(bf16)
    return high, low


def rotate_kernel(core_ref, template_ref, map_ref, out_ref, normed_ref, index_ref):
    values = template_ref[...]
    centred = values - jnp.sum(values) / voxels
    normed = centred / jnp.sqrt(jnp.sum(centred * centred) + epsilon)
    normed_ref[...] = jnp.zeros_like(normed_ref)
    for a in range(edge):
        at = slice(edge * (a // 5), edge * (a // 5 + 1))
        normed_ref[at, edge * (a % 5) : edge * (a % 5 + 1)] = normed[a]
    index_ref[...] = jnp.full_like(index_ref, -1)

    for core in range(2):

        @pl.when(core_ref[0] == core)
        def place():
            for a in range(edge):
                for b in range(half):
                    start = (a * edge + half * core + b) * edge
                    at = half * (a // 5) + b
                    index_ref[at : at + 1, edge * (a % 5) : edge * (a % 5 + 1)] = map_ref[
                        0:1, start : start + edge
                    ]

    def gather(i, carry):
        at = pl.ds(pl.multiple_of(8 * i, 8), 8)
        index = index_ref[at, :]
        source = jnp.maximum(index, 0)
        a = source // (edge * edge)
        rest = source - a * (edge * edge)
        b = rest // edge
        c = rest - b * edge
        group = a // 5
        lane = (a - 5 * group) * edge + c
        high = jnp.where(index < 0, -1, group * edge + b)
        totals = [jnp.zeros((8, 128), f32) for _ in range(4)]
        for row in range(5 * edge):
            table = jnp.broadcast_to(normed_ref[row : row + 1, :], (8, 128))
            found = jnp.take_along_axis(table, lane, axis=1, mode="promise_in_bounds")
            totals[row % 4] = jnp.where(high == row, found, totals[row % 4])
        out_ref[at, :] = (totals[0] + totals[1]) + (totals[2] + totals[3])
        return carry

    lax.fori_loop(0, 8, gather, 0, unroll=2)


def whiten_kernel(
    place_ref, rows_ref, fh_hbm, fl_hbm, bh_hbm, bl_hbm, own_ref, out_ref, x_ref, fh_ref, fl_ref, bh_ref, bl_ref, sems
):
    column = place_ref[0]
    copies = [
        pltpu.make_async_copy(fh_hbm, fh_ref, sems.at[0]),
        pltpu.make_async_copy(fl_hbm, fl_ref, sems.at[1]),
        pltpu.make_async_copy(bh_hbm.at[column], bh_ref, sems.at[2]),
        pltpu.make_async_copy(bl_hbm.at[column], bl_ref, sems.at[3]),
    ]
    for copy in copies:
        copy.start()
    out_ref[0, 2 * rows :, :] = own_ref[:half_rows, :]
    for plane in range(2):
        for j in range(length // cols):
            x_ref[rows * plane : rows * (plane + 1), cols * j : cols * (j + 1)] = rows_ref[
                plane * 8 + j
            ]
    xh, xl = split(x_ref[...])
    copies[0].wait()
    spec = lax.dot_general(fh_ref[...], xh, nt, preferred_element_type=f32) + lax.dot_general(
        fh_ref[...], xl, nt, preferred_element_type=f32
    )
    copies[1].wait()
    spec = spec + lax.dot_general(fl_ref[...], xh, nt, preferred_element_type=f32)
    real = spec[:freq_pad]
    imag = spec[freq_pad:]
    power = real * real + imag * imag
    k = lax.broadcasted_iota(jnp.int32, power.shape, 0)
    before = jnp.where(k == 0, power[1:2], pltpu.roll(power, 1, 0))
    after = jnp.where(k == freqs - 1, power[freqs - 2 : freqs - 1], pltpu.roll(power, freq_pad - 1, 0))
    total = 2.0 * jnp.sum(power, axis=0, keepdims=True) - power[0:1] - power[freqs - 1 : freqs]
    smoothed = (before + power + after) / 3.0 + floor_share * (total / length) + epsilon
    weights = lax.rsqrt(smoothed)
    wh, wl = split(jnp.concatenate([real * weights, imag * weights], axis=0))
    copies[2].wait()
    copies[3].wait()
    out_ref[0, : 2 * rows, :] = (
        lax.dot_general(wh, bh_ref[...], tn, preferred_element_type=f32)
        + lax.dot_general(wl, bh_ref[...], tn, preferred_element_type=f32)
        + lax.dot_general(wh, bl_ref[...], tn, preferred_element_type=f32)
    )


def match_kernel(
    where_ref, own_hbm, other_hbm, mine_ref, theirs_ref, scale_ref, g_ref, v_ref, t_ref, l_ref, w_ref, acc_ref, best_ref, score_ref, sems
):
    z0 = where_ref[0]
    ylo = where_ref[1]
    core = where_ref[2]
    first = (core == 0).astype(f32)
    copies = [
        pltpu.make_async_copy(own_hbm, g_ref.at[core], sems.at[0]),
        pltpu.make_async_copy(other_hbm, g_ref.at[1 - core], sems.at[1]),
    ]
    for copy in copies:
        copy.start()
    for copy in copies:
        copy.wait()

    def load_plane(j, energy):
        plane = z0 - half + j
        valid = jnp.logical_and(plane >= 0, plane < planes).astype(f32)
        plane = jnp.clip(plane, 0, planes - 1)
        z = plane % 16
        start = pl.multiple_of((plane // 16) * rows, rows)
        v_ref[j, half : half + rows, :] = g_ref[core, z, pl.ds(start, rows), :] * valid
        v_ref[j, 0:half, :] = g_ref[0, z, pl.ds(start, rows), :][rows - half :] * (valid * (1.0 - first))
        v_ref[j, half + rows : 56, :] = g_ref[1, z, pl.ds(start, rows), :][:half] * (valid * first)
        full = v_ref[j]
        v_ref[j] = pltpu.roll(full, (j % 4) * 32, 1)
        inside = jnp.logical_and(j >= 16 * ylo, j < 16 * ylo + edge).astype(f32)
        return energy + full * full * inside

    energy = lax.fori_loop(0, span, load_plane, jnp.zeros((56, window), f32), unroll=4)

    lane = lax.broadcasted_iota(jnp.int32, (blocks, window), 1)
    cell = lax.broadcasted_iota(jnp.int32, (half, window), 1)

    t_ref[...] = jnp.zeros_like(t_ref)

    def widen(r, carry):
        for core_half in range(2):
            for quad in range(6):
                total = jnp.zeros((half, window), f32)
                for part in range(4):
                    a = 4 * quad + part
                    at = 2 * rows + half * (a // 5)
                    source = g_ref[core_half, r, at : at + half, :]
                    moved = pltpu.roll(source, (32 * part - edge * (a % 5)) % window, 1)
                    keep = jnp.logical_and(cell >= 32 * part, cell < 32 * part + edge)
                    total = jnp.where(keep, moved, total)
                t_ref[r, quad, 1 + half * core_half : 1 + half * (core_half + 1), :] = total
        return carry

    lax.fori_loop(0, rots, widen, 0, unroll=2)

    def expand(u, carry):
        here = pl.ds(pl.multiple_of(u * blocks, blocks), blocks)
        for parity in range(2):
            for quad in range(span // 4):
                total = None
                for part in range(4):
                    row = jnp.broadcast_to(v_ref[4 * quad + part, pl.ds(2 * u + parity, 1), :], (blocks, window))
                    moved = pltpu.roll(row, 8, 1, stride=8, stride_axis=0)
                    total = moved if total is None else jnp.where(lane >= 32 * part, moved, total)
                high, low = split(total)
                for k, piece in enumerate((high, low, high)):
                    at = window * (6 * quad + 3 * parity + k)
                    l_ref[here, at : at + window] = piece
        return carry

    lax.fori_loop(0, 28, expand, 0, unroll=2)

    def build(v, slot):
        for tap, targets in ((-1, ((0, 1),)), (0, ((0, 0), (1, 1))), (1, ((1, 0),))):
            for pair in range(rots // 2):
                for quad in range(6):
                    moved = []
                    for r in (2 * pair, 2 * pair + 1):
                        row = t_ref[r, quad, pl.ds(2 * v + tap + 1, 1), :]
                        moved.append(pltpu.roll(jnp.broadcast_to(row, (8, window)), 0, 1, stride=1, stride_axis=0))
                    high, low = split(jnp.concatenate(moved, axis=0))
                    for parity, p in targets:
                        for k, piece in enumerate((high, high, low)):
                            at = window * (6 * quad + 3 * parity + k)
                            place = 128 * p + 16 * pair
                            w_ref[slot, place : place + 16, at : at + window] = piece

    def product(v, slot):
        here = pl.ds(pl.multiple_of(v * blocks, blocks), 16 * blocks)
        left = jnp.concatenate([l_ref[here, : 6 * depth], l_ref[here, 4 * depth : 10 * depth]], axis=0)
        acc_ref[...] += lax.dot_general(left, w_ref[slot], nt, preferred_element_type=f32)

    acc_ref[...] = jnp.zeros_like(acc_ref)
    build(0, 0)

    def step(i, carry):
        build(2 * i + 1, 1)
        product(2 * i, 0)
        build(2 * i + 2, 0)
        product(2 * i + 1, 1)
        return carry

    lax.fori_loop(0, 6, step, 0)
    product(12, 0)

    lanes = lax.broadcasted_iota(jnp.int32, (16, window), 1)
    for p in range(2):
        best = acc_ref[:, 128 * p : 128 * (p + 1)]
        for shift in (64, 32, 16, 8):
            best = jnp.maximum(best, pltpu.roll(best, shift, 1))
        best_ref[...] = best
        for plane in range(2):
            score = jnp.zeros((16, window), f32)
            for block in range(13):
                found = best_ref[pl.ds(256 * plane + blocks - 1 - block, 16, stride=blocks), :]
                score = jnp.where(lanes // 8 == block, found, score)
            score_ref[pl.ds(rows * plane + p, 16, stride=2), :] = score
    mine_ref[...] = score_ref[pl.ds(pl.multiple_of(rows * ylo, rows), rows), :][:, :cols]
    theirs_ref[...] = score_ref[pl.ds(pl.multiple_of(rows * (1 - ylo), rows), rows), :][:, :cols]

    def shifted(values, count):
        return pltpu.roll(values, values.shape[0] - count, 0)

    sums = energy
    for count in (1, 2, 4):
        sums = sums + shifted(sums, count)
    sums = sums + shifted(sums, 8) + shifted(sums, 16)
    sums = sums[:rows]
    for count in (1, 2, 4):
        sums = sums + pltpu.roll(sums, window - count, 1)
    sums = sums + pltpu.roll(sums, window - 8, 1) + pltpu.roll(sums, window - 16, 1)
    scale_ref[...] = lax.rsqrt(sums / voxels + epsilon)[:, :cols]


def match_scratch():
    return [
        pltpu.VMEM((2, 16, shard_rows, 128), f32),
        pltpu.VMEM((span, 56, window), f32),
        pltpu.VMEM((rots, 6, 32, window), f32),
        pltpu.VMEM((28 * blocks, 10 * depth), bf16),
        pltpu.VMEM((2, 256, 6 * depth), bf16),
        pltpu.VMEM((32 * blocks, 256), f32),
        pltpu.VMEM((32 * blocks, 128), f32),
        pltpu.VMEM((2 * rows, 128), f32),
        pltpu.SemaphoreType.DMA((2,)),
    ]


def shards(volume, template, voxel_maps):
    ylo, z, core = lax.axis_index("ylo"), lax.axis_index("z"), lax.axis_index("core")
    column = lax.axis_index("x") * 2 + lax.axis_index("yhi")
    vmem = pl.BlockSpec(memory_space=pltpu.VMEM)
    hbm = pl.BlockSpec(memory_space=pl.ANY)
    smem = pl.BlockSpec(memory_space=pltpu.SMEM)

    copies = jnp.broadcast_to(volume, (16, rows, cols))
    full_rows = lax.all_to_all(copies, group, split_axis=0, concat_axis=0, tiled=True)

    own = pl.pallas_call(
        rotate_kernel,
        out_shape=jax.ShapeDtypeStruct((64, 128), f32),
        grid_spec=pltpu.PrefetchScalarGridSpec(
            num_scalar_prefetch=1,
            grid=(1,),
            in_specs=[
                pl.BlockSpec((edge, edge, edge), lambda i, c: (0, 0, 0)),
                pl.BlockSpec((1, voxels), lambda i, c: (0, 0)),
            ],
            out_specs=pl.BlockSpec((64, 128), lambda i, c: (0, 0)),
            scratch_shapes=[pltpu.VMEM((5 * edge, 128), f32), pltpu.VMEM((64, 128), jnp.int32)],
        ),
        name="rotate",
    )(core[None].astype(jnp.int32), template, voxel_maps)

    tables = [jnp.asarray(table) for table in dft_tables()]
    shard = pl.pallas_call(
        whiten_kernel,
        out_shape=jax.ShapeDtypeStruct((1, shard_rows, 128), f32),
        grid_spec=pltpu.PrefetchScalarGridSpec(
            num_scalar_prefetch=1,
            grid=(1,),
            in_specs=[
                pl.BlockSpec((16, rows, cols), lambda i, c: (0, 0, 0)),
                hbm,
                hbm,
                hbm,
                hbm,
                pl.BlockSpec((64, 128), lambda i, c: (0, 0)),
            ],
            out_specs=pl.BlockSpec((1, shard_rows, 128), lambda i, c: (0, 0, 0)),
            scratch_shapes=[
                pltpu.VMEM((2 * rows, length), f32),
                pltpu.VMEM((2 * freq_pad, length), bf16),
                pltpu.VMEM((2 * freq_pad, length), bf16),
                pltpu.VMEM((2 * freq_pad, window), bf16),
                pltpu.VMEM((2 * freq_pad, window), bf16),
                pltpu.SemaphoreType.DMA((4,)),
            ],
        ),
        compiler_params=pltpu.CompilerParams(vmem_limit_bytes=60 * 2**20),
        name="whiten",
    )(column[None].astype(jnp.int32), full_rows, *tables, own)

    gathered = lax.all_gather(shard, "z", axis=0, tiled=True)
    partner = lax.ppermute(gathered, "core", [(0, 1), (1, 0)])
    place = jnp.stack([z, ylo, core]).astype(jnp.int32)
    mine, theirs, scale = pl.pallas_call(
        match_kernel,
        out_shape=[jax.ShapeDtypeStruct((rows, cols), f32)] * 3,
        in_specs=[smem, hbm, hbm],
        out_specs=[vmem] * 3,
        scratch_shapes=match_scratch(),
        compiler_params=pltpu.CompilerParams(vmem_limit_bytes=56 * 2**20),
        name="match",
    )(place, gathered, partner)
    received = lax.ppermute(theirs, "ylo", [(0, 1), (1, 0)])
    return (jnp.maximum(mine, received) * scale)[None]


def solution(mesh):
    inner = Mesh(mesh.devices.reshape(2, 16, 2, 4, 2), ("ylo", "z", "core", "x", "yhi"))
    orient, bricks = ("ylo", "z"), ("x", "yhi")
    return jax.shard_map(
        shards,
        mesh=inner,
        in_specs=(P(orient, "core", bricks), P(), P(orient, None)),
        out_specs=P(orient, "core", bricks),
        check_vma=False,
    )
```

time: 190 us -> 110 us (0.58)
  waiting for transfers between devices: 101 us -> 7.48 us
  blocking collectives: 0 us -> 35.9 us
  between operations: 13.5 us -> 0.06 us
  local copies, waits for them, and re-layouts: 14.7 us -> 4.09 us
  starting transfers between devices: 10.6 us -> 20.5 us
  Pallas kernels: 46.5 us -> 39.9 us
    all_gather x2 -> x0, waiting for transfers between devices: 101 us -> none  [the longest x1 68.7 us: shards(): gathered = lax.all_gather(shard, 'z', axis=0, tiled=True)]
    all_gather x0 -> x1, blocking collectives: none -> 35.9 us  [shards(): gathered = lax.all_gather(shard, 'z', axis=0, tiled=True)]
    ppermute x1 -> x2, starting transfers between devices: 4.02 us -> 13 us  [the longest x1 10.5 us: shards(): partner = lax.ppermute(gathered, 'core', [(0, 1), (1, 0)])]
    pallas_call x3, Pallas kernels: 46.5 us -> 39.9 us  [the longest x1 30.4 us: shards(): pl.pallas_call(match_kernel, out_shape=[jax.ShapeDtypeStruct((rows, cols)...]
    reshape x4 -> x0, local copies, waits for them, and re-layouts: 5.58 us -> none  [the longest x2 2.08 us: shards(): maps = voxel_maps.reshape(2, half, edge, edge)]
    unnamed x16 -> x4, local copies, waits for them, and re-layouts: 6.28 us -> 0.71 us
    ppermute x1 -> x2, waiting for transfers between devices: 0.01 us -> 3.82 us  [the longest x1 2.26 us: shards(): received = lax.ppermute(theirs, 'ylo', [(0, 1), (1, 0)])]
    all_to_all x1, waiting for transfers between devices: 0.01 us -> 3.66 us  [shards(): lax.all_to_all(copies, group, split_axis=0, concat_axis=0, tiled=True)]
  transfers between devices with their start and end apart: 4 -> 3, of which waited for: 2 -> 3; matrix products, arithmetic and copies ran while one was open for 2% -> 1% of each run, Pallas kernels for 8% -> 4%
where the time goes in v2:
time: 110 us
  Pallas kernels  39.9 us (36%)
  blocking collectives  35.9 us (33%)
  starting transfers between devices  20.5 us (19%)
  waiting for transfers between devices  7.48 us (7%)
  local copies, waits for them, and re-layouts  4.09 us (4%)
  other arithmetic  2 us (2%)
    all_gather x1, blocking collectives, shards(): gathered = lax.all_gather(shard, 'z', axis=0, tiled=True)  35.9 us
    pallas_call x1, Pallas kernels, shards(): pl.pallas_call(match_kernel, out_shape=[jax.ShapeDtypeStruct((rows, cols)...  30.4 us
    ppermute x1, starting transfers between devices, shards(): partner = lax.ppermute(gathered, 'core', [(0, 1), (1, 0)])  10.5 us
    all_to_all x1, starting transfers between devices, shards(): lax.all_to_all(copies, group, split_axis=0, concat_axis=0, tiled=True)  7.58 us
    pallas_call x1, Pallas kernels, shards(): pl.pallas_call(whiten_kernel, out_shape=jax.ShapeDtypeStruct((1, shard_ro...  5.46 us
    pallas_call x1, Pallas kernels, shards(): pl.pallas_call(rotate_kernel, out_shape=jax.ShapeDtypeStruct((64, 128), f...  3.99 us
    all_to_all x1, waiting for transfers between devices, shards(): lax.all_to_all(copies, group, split_axis=0, concat_axis=0, tiled=True)  3.66 us
    ppermute x1, starting transfers between devices, shards(): received = lax.ppermute(theirs, 'ylo', [(0, 1), (1, 0)])  2.42 us
  transfers between devices with their start and end apart: 3, of which 3 were waited for; matrix products, arithmetic and copies ran while one was open for 1% of the time, Pallas kernels for 4%

profile of v2, /device:TPU:1, one launch (start us, length us, event | category | flops | bytes accessed | tf_op | source)
XLA Modules:
  0.0 109.9 jit_solution(2053721982495320676)
XLA Ops:
  0.0 1.4 %broadcast_in_dim.16 = f32[16,32,104]{2,1,0:T(8,128)} broadcast(f32[32,104]{1,0:T(8,128)} %bitcast.7), dimensions={1,2} | broadcast | bytes 226304 | tf_op jit(solution)/shard_map/broadcast_in_dim | solution.py:310
  1.4 7.6 %all-to-all-start = ((f32[16,32,104]{2,1,0:T(8,128)}), f32[16,32,104]{2,1,0:T(8,128)S(1)}, u32[]{:S(2)}, u32[]{:S(2)}) async-start(f32[16,32,104]{2,1,0:T(8,128)} %broadcast_in_dim.16), calls=%async_computation | async-start | bytes 524288 | tf_op jit(solution)/shard_map/all_to_all | solution.py:311
  9.0 4.0 %rotate.1.own_ref = f32[64,128]{1,0:T(8,128)} custom-call(s32[1]{0:T(128)} %bitcast.2.core_ref, f32[24,24,24]{2,1,0:T(8,128)} %template_ref.1, s32[1,13824]{1,0:T(1,128)} %map_ref.1), custom_call_target="tpu_custom_call" | custom-call | tf_op jit(solution)/shard_map/rotate/pallas_call | solution.py:313
  13.0 3.7 %all-to-all-done.rows_ref = f32[16,32,104]{2,1,0:T(8,128)S(1)} async-done(((f32[16,32,104]{2,1,0:T(8,128)}), f32[16,32,104]{2,1,0:T(8,128)S(1)}, u32[]{:S(2)}, u32[]{:S(2)}) %all-to-all-start) | async-done | bytes 213024 | tf_op jit(solution)/shard_map/all_to_all | solution.py:311
  16.7 0.0 copy-start.1
  16.7 0.7 copy-done.1
  17.4 5.5 %whiten.1 = f32[1,124,128]{2,1,0:T(8,128)} custom-call(s32[1]{0:T(128)} %bitcast.3.place_ref, f32[16,32,104]{2,1,0:T(8,128)} %copy-done.1, bf16[864,832]{1,0:T(8,128)(2,1)} %constant.30.clone.fh_hbm, bf16[864,832]{1,0:T(8,128)(2,1)} %constant.31.clone.fl_hbm, bf16[8,864,128]{2,1,0:T(8,128)(2,1)} %constant.32.clone.bh_hbm, ...), custom_call_target="tpu_custom_call" | custom-call | tf_op jit(solution)/shard_map/whiten/pallas_call | solution.py:330
  22.9 35.9 %all_gather.3.own_hbm = f32[16,124,128]{2,1,0:T(8,128)S(1)} all-gather(f32[1,124,128]{2,1,0:T(8,128)} %whiten.1), channel_id=1, replica_groups=mesh['ylo'=2,'z'=16,'core'=2,'x'=4,'yhi'=2] {'z'}, dimensions={0}, use_global_device_ids=true | all-gather | bytes 1079296 | tf_op jit(solution)/shard_map/all_gather | solution.py:358
  58.7 0.0 copy-start
  58.7 0.6 copy.8
  59.3 10.5 %collective-permute-start = (f32[16,124,128]{2,0,1:T(8,128)S(1)}, f32[16,124,128]{2,0,1:T(8,128)S(1)}, u32[]{:S(2)}, u32[]{:S(2)}) collective-permute-start(f32[16,124,128]{2,0,1:T(8,128)S(1)} %copy.8), channel_id=1, source_target_pairs={{0,8},{8,0},{1,9},{9,1},{2,10},{10,2},{3,11},{11,3},{4,12},{12,4},... | collective-permute-start | bytes 3047432 | tf_op jit(solution)/shard_map/ppermute | solution.py:359
  69.9 0.7 pad_add_fusion.where_ref
  70.5 1.6 %collective-permute-done = f32[16,124,128]{2,0,1:T(8,128)S(1)} collective-permute-done((f32[16,124,128]{2,0,1:T(8,128)S(1)}, f32[16,124,128]{2,0,1:T(8,128)S(1)}, u32[]{:S(2)}, u32[]{:S(2)}) %collective-permute-start) | collective-permute-done | bytes 1015840 | tf_op jit(solution)/shard_map/ppermute | solution.py:359
  72.1 1.4 %copy.9.other_hbm = f32[16,124,128]{2,1,0:T(8,128)} copy(f32[16,124,128]{2,0,1:T(8,128)S(1)} %collective-permute-done) | data formatting | bytes 2031616 | tf_op jit(solution)/shard_map/ppermute | solution.py:359
  73.4 0.0 copy-done
  73.4 30.4 %match.1 = (f32[32,104]{1,0:T(8,128)}, f32[32,104]{1,0:T(8,128)}, f32[32,104]{1,0:T(8,128)}) custom-call(s32[3]{0:T(128)} %pad_add_fusion.where_ref, f32[16,124,128]{2,1,0:T(8,128)} %copy-done, f32[16,124,128]{2,1,0:T(8,128)} %copy.9.other_hbm), custom_call_target="tpu_custom_call" | custom-call | tf_op jit(solution)/shard_map/match/pallas_call | solution.py:361
  103.9 2.4 %collective-permute-start.1 = (f32[32,104]{1,0:T(8,128)}, f32[32,104]{1,0:T(8,128)S(1)}, u32[]{:S(2)}, u32[]{:S(2)}) collective-permute-start(f32[32,104]{1,0:T(8,128)} %get-tuple-element.9), channel_id=1, source_target_pairs={{0,256},{256,0},{1,257},{257,1},{2,258},{258,2},{3,259},{259,3},{4... | collective-permute-start | bytes 39944 | tf_op jit(solution)/shard_map/ppermute | solution.py:370
  106.3 2.3 %collective-permute-done.1 = f32[32,104]{1,0:T(8,128)S(1)} collective-permute-done((f32[32,104]{1,0:T(8,128)}, f32[32,104]{1,0:T(8,128)S(1)}, u32[]{:S(2)}, u32[]{:S(2)}) %collective-permute-start.1) | collective-permute-done | bytes 13344 | tf_op jit(solution)/shard_map/ppermute | solution.py:370
  108.6 1.3 %multiply_bitcast_fusion = f32[1,32,104]{2,1,0:T(8,128)} fusion(f32[32,104]{1,0:T(8,128)} %get-tuple-element.10, f32[32,104]{1,0:T(8,128)} %get-tuple-element.8, f32[32,104]{1,0:T(8,128)S(1)} %collective-permute-done.1), kind=kLoop, calls=%fused_computation | loop fusion | flops 6656 | bytes 53248 | tf_op jit(solution)/shard_map/broadcast_in_dim | solution.py:371
Async XLA Ops:
  1.4 15.3 %all-to-all-start = ((f32[16,32,104]{2,1,0:T(8,128)}), f32[16,32,104]{2,1,0:T(8,128)S(1)}, u32[]{:S(2)}, u32[]{:S(2)}) async-start(f32[16,32,104]{2,1,0:T(8,128)} %broadcast_in_dim.16), calls=%async_computation | async-start | bytes 524288 | tf_op jit(solution)/shard_map/all_to_all | solution.py:311
  16.7 0.7 copy-start.1
  58.7 14.7 %copy-start = (f32[16,124,128]{2,1,0:T(8,128)}, f32[16,124,128]{2,1,0:T(8,128)S(1)}, u32[]{:S(2)}) copy-start(f32[16,124,128]{2,1,0:T(8,128)S(1)} %all_gather.3.own_hbm) | copy-start | bytes 3047428
  59.3 12.8 %collective-permute-start = (f32[16,124,128]{2,0,1:T(8,128)S(1)}, f32[16,124,128]{2,0,1:T(8,128)S(1)}, u32[]{:S(2)}, u32[]{:S(2)}) collective-permute-start(f32[16,124,128]{2,0,1:T(8,128)S(1)} %copy.8), channel_id=1, source_target_pairs={{0,8},{8,0},{1,9},{9,1},{2,10},{10,2},{3,11},{11,3},{4,12},{12,4},... | collective-permute-start | bytes 3047432 | tf_op jit(solution)/shard_map/ppermute | solution.py:359
  103.9 4.7 %collective-permute-start.1 = (f32[32,104]{1,0:T(8,128)}, f32[32,104]{1,0:T(8,128)S(1)}, u32[]{:S(2)}, u32[]{:S(2)}) collective-permute-start(f32[32,104]{1,0:T(8,128)} %get-tuple-element.9), channel_id=1, source_target_pairs={{0,256},{256,0},{1,257},{257,1},{2,258},{258,2},{3,259},{259,3},{4... | collective-permute-start | bytes 39944 | tf_op jit(solution)/shard_map/ppermute | solution.py:370

commit v3 on v2

--- a/solution.py
+++ b/solution.py
@@ -24,7 +24,7 @@
 freqs = length // 2 + 1
 freq_pad = 432
 group = "ylo", "x", "yhi"
-half_rows = 60
+half_rows = 56
 shard_rows = 2 * rows + half_rows
 span = planes // 2 + edge
 rots = 16
@@ -57,13 +57,23 @@
     padded = padded.reshape(2 * freq_pad, length + edge)
     bricks = length // cols
     backward = np.stack([padded[:, cols * j : cols * j + window] for j in range(bricks)])
-    return split_table(forward) + split_table(backward)
+    return np.stack(split_table(forward)), np.stack(split_table(backward))
 
 
 def split(values):
     high = values.astype(bf16)
     low = (values - high.astype(f32)).astype(bf16)
     return high, low
+
+
+def cells_of(a, b):
+    if a < 20:
+        return [(half * (a // 5) + b, edge * (a % 5), 0, edge)]
+    if b < 8:
+        return [(48 + b, edge * (a - 20), 0, edge)]
+    if a < 22:
+        return [(48 + 4 * (a - 20) + b - 8, 96, 0, edge)]
+    return [(half * j + b - 4 * (a - 22), 120, 8 * j, 8) for j in range(3)]
 
 
 def rotate_kernel(core_ref, template_ref, map_ref, out_ref, normed_ref, index_ref):
@@ -83,10 +93,10 @@
             for a in range(edge):
                 for b in range(half):
                     start = (a * edge + half * core + b) * edge
-                    at = half * (a // 5) + b
-                    index_ref[at : at + 1, edge * (a % 5) : edge * (a % 5 + 1)] = map_ref[
-                        0:1, start : start + edge
-                    ]
+                    for at, lane, first, width in cells_of(a, b):
+                        index_ref[at : at + 1, lane : lane + width] = map_ref[
+                            0:1, start + first : start + first + width
+                        ]
 
     def gather(i, carry):
         at = pl.ds(pl.multiple_of(8 * i, 8), 8)
@@ -107,22 +117,22 @@
         out_ref[at, :] = (totals[0] + totals[1]) + (totals[2] + totals[3])
         return carry
 
-    lax.fori_loop(0, 8, gather, 0, unroll=2)
+    lax.fori_loop(0, half_rows // 8, gather, 0, unroll=7)
 
 
 def whiten_kernel(
-    place_ref, rows_ref, fh_hbm, fl_hbm, bh_hbm, bl_hbm, own_ref, out_ref, x_ref, fh_ref, fl_ref, bh_ref, bl_ref, sems
+    place_ref, rows_ref, f_hbm, b_hbm, own_ref, out_ref, x_ref, fh_ref, fl_ref, bh_ref, bl_ref, sems
 ):
     column = place_ref[0]
     copies = [
-        pltpu.make_async_copy(fh_hbm, fh_ref, sems.at[0]),
-        pltpu.make_async_copy(fl_hbm, fl_ref, sems.at[1]),
-        pltpu.make_async_copy(bh_hbm.at[column], bh_ref, sems.at[2]),
-        pltpu.make_async_copy(bl_hbm.at[column], bl_ref, sems.at[3]),
+        pltpu.make_async_copy(f_hbm.at[0], fh_ref, sems.at[0]),
+        pltpu.make_async_copy(f_hbm.at[1], fl_ref, sems.at[1]),
+        pltpu.make_async_copy(b_hbm.at[0, column], bh_ref, sems.at[2]),
+        pltpu.make_async_copy(b_hbm.at[1, column], bl_ref, sems.at[3]),
     ]
     for copy in copies:
         copy.start()
-    out_ref[0, 2 * rows :, :] = own_ref[:half_rows, :]
+    out_ref[0, 2 * rows :, :] = own_ref[...]
     for plane in range(2):
         for j in range(length // cols):
             x_ref[rows * plane : rows * (plane + 1), cols * j : cols * (j + 1)] = rows_ref[
@@ -155,20 +165,12 @@
 
 
 def match_kernel(
-    where_ref, own_hbm, other_hbm, mine_ref, theirs_ref, scale_ref, g_ref, v_ref, t_ref, l_ref, w_ref, acc_ref, best_ref, score_ref, sems
+    where_ref, own_ref, other_ref, mine_ref, theirs_ref, scale_ref, v_ref, t_ref, l_ref, w_ref, acc_ref, best_ref, score_ref
 ):
     z0 = where_ref[0]
     ylo = where_ref[1]
     core = where_ref[2]
     first = (core == 0).astype(f32)
-    copies = [
-        pltpu.make_async_copy(own_hbm, g_ref.at[core], sems.at[0]),
-        pltpu.make_async_copy(other_hbm, g_ref.at[1 - core], sems.at[1]),
-    ]
-    for copy in copies:
-        copy.start()
-    for copy in copies:
-        copy.wait()
 
     def load_plane(j, energy):
         plane = z0 - half + j
@@ -176,9 +178,10 @@
         plane = jnp.clip(plane, 0, planes - 1)
         z = plane % 16
         start = pl.multiple_of((plane // 16) * rows, rows)
-        v_ref[j, half : half + rows, :] = g_ref[core, z, pl.ds(start, rows), :] * valid
-        v_ref[j, 0:half, :] = g_ref[0, z, pl.ds(start, rows), :][rows - half :] * (valid * (1.0 - first))
-        v_ref[j, half + rows : 56, :] = g_ref[1, z, pl.ds(start, rows), :][:half] * (valid * first)
+        near = other_ref[z, pl.ds(start, rows), :]
+        v_ref[j, half : half + rows, :] = own_ref[z, pl.ds(start, rows), :] * valid
+        v_ref[j, 0:half, :] = near[rows - half :] * (valid * (1.0 - first))
+        v_ref[j, half + rows : 56, :] = near[:half] * (valid * first)
         full = v_ref[j]
         v_ref[j] = pltpu.roll(full, (j % 4) * 32, 1)
         inside = jnp.logical_and(j >= 16 * ylo, j < 16 * ylo + edge).astype(f32)
@@ -187,25 +190,41 @@
     energy = lax.fori_loop(0, span, load_plane, jnp.zeros((56, window), f32), unroll=4)
 
     lane = lax.broadcasted_iota(jnp.int32, (blocks, window), 1)
+    place = lax.broadcasted_iota(jnp.int32, (blocks, window), 0)
+    owner = ((lane + 8 * place + 8) & (window - 1)) // 32
     cell = lax.broadcasted_iota(jnp.int32, (half, window), 1)
 
     t_ref[...] = jnp.zeros_like(t_ref)
 
-    def widen(r, carry):
-        for core_half in range(2):
-            for quad in range(6):
-                total = jnp.zeros((half, window), f32)
-                for part in range(4):
-                    a = 4 * quad + part
-                    at = 2 * rows + half * (a // 5)
-                    source = g_ref[core_half, r, at : at + half, :]
-                    moved = pltpu.roll(source, (32 * part - edge * (a % 5)) % window, 1)
-                    keep = jnp.logical_and(cell >= 32 * part, cell < 32 * part + edge)
-                    total = jnp.where(keep, moved, total)
-                t_ref[r, quad, 1 + half * core_half : 1 + half * (core_half + 1), :] = total
-        return carry
-
-    lax.fori_loop(0, rots, widen, 0, unroll=2)
+    def widen(sources):
+        def placed(total, source, lane_from, lane_to, width):
+            moved = pltpu.roll(source, (lane_to - lane_from) % window, 1)
+            at = cell[: source.shape[0]]
+            return jnp.where(jnp.logical_and(at >= lane_to, at < lane_to + width), moved, total)
+
+        def step(r, carry):
+            for k, source_ref in enumerate(sources):
+                put = 1 + half * k
+                for quad in range(6):
+                    for low, high in ((0, 8), (8, half)) if quad == 5 else ((0, half),):
+                        total = jnp.zeros((high - low, window), f32)
+                        for part in range(4):
+                            for at, lane_from, c, width in cells_of(4 * quad + part, low):
+                                at = 2 * rows + at
+                                source = source_ref[r, at : at + high - low, :]
+                                total = placed(total, source, lane_from, 32 * part + c, width)
+                        t_ref[r, quad, put + low : put + high, :] = total
+            return carry
+
+        lax.fori_loop(0, rots, step, 0, unroll=2)
+
+    @pl.when(core == 0)
+    def from_first():
+        widen((own_ref, other_ref))
+
+    @pl.when(core != 0)
+    def from_second():
+        widen((other_ref, own_ref))
 
     def expand(u, carry):
         here = pl.ds(pl.multiple_of(u * blocks, blocks), blocks)
@@ -214,15 +233,15 @@
                 total = None
                 for part in range(4):
                     row = jnp.broadcast_to(v_ref[4 * quad + part, pl.ds(2 * u + parity, 1), :], (blocks, window))
-                    moved = pltpu.roll(row, 8, 1, stride=8, stride_axis=0)
-                    total = moved if total is None else jnp.where(lane >= 32 * part, moved, total)
+                    total = row if total is None else jnp.where(owner >= part, row, total)
+                total = pltpu.roll(total, 8, 1, stride=8, stride_axis=0)
                 high, low = split(total)
                 for k, piece in enumerate((high, low, high)):
                     at = window * (6 * quad + 3 * parity + k)
                     l_ref[here, at : at + window] = piece
         return carry
 
-    lax.fori_loop(0, 28, expand, 0, unroll=2)
+    lax.fori_loop(0, 28, expand, 0, unroll=4)
 
     def build(v, slot):
         for tap, targets in ((-1, ((0, 1),)), (0, ((0, 0), (1, 1))), (1, ((1, 0),))):
@@ -288,7 +307,6 @@
 
 def match_scratch():
     return [
-        pltpu.VMEM((2, 16, shard_rows, 128), f32),
         pltpu.VMEM((span, 56, window), f32),
         pltpu.VMEM((rots, 6, 32, window), f32),
         pltpu.VMEM((28 * blocks, 10 * depth), bf16),
@@ -296,7 +314,6 @@
         pltpu.VMEM((32 * blocks, 256), f32),
         pltpu.VMEM((32 * blocks, 128), f32),
         pltpu.VMEM((2 * rows, 128), f32),
-        pltpu.SemaphoreType.DMA((2,)),
     ]
 
 
@@ -304,7 +321,7 @@
     ylo, z, core = lax.axis_index("ylo"), lax.axis_index("z"), lax.axis_index("core")
     column = lax.axis_index("x") * 2 + lax.axis_index("yhi")
     vmem = pl.BlockSpec(memory_space=pltpu.VMEM)
-    hbm = pl.BlockSpec(memory_space=pl.ANY)
+    hbm = pl.BlockSpec(memory_space=pltpu.HBM)
     smem = pl.BlockSpec(memory_space=pltpu.SMEM)
 
     copies = jnp.broadcast_to(volume, (16, rows, cols))
@@ -312,17 +329,11 @@
 
     own = pl.pallas_call(
         rotate_kernel,
-        out_shape=jax.ShapeDtypeStruct((64, 128), f32),
-        grid_spec=pltpu.PrefetchScalarGridSpec(
-            num_scalar_prefetch=1,
-            grid=(1,),
-            in_specs=[
-                pl.BlockSpec((edge, edge, edge), lambda i, c: (0, 0, 0)),
-                pl.BlockSpec((1, voxels), lambda i, c: (0, 0)),
-            ],
-            out_specs=pl.BlockSpec((64, 128), lambda i, c: (0, 0)),
-            scratch_shapes=[pltpu.VMEM((5 * edge, 128), f32), pltpu.VMEM((64, 128), jnp.int32)],
-        ),
+        out_shape=jax.ShapeDtypeStruct((half_rows, 128), f32),
+        in_specs=[smem, vmem, vmem],
+        out_specs=vmem,
+        scratch_shapes=[pltpu.VMEM((5 * edge, 128), f32), pltpu.VMEM((half_rows, 128), jnp.int32)],
+        compiler_params=pltpu.CompilerParams(vmem_limit_bytes=8 * 2**20),
         name="rotate",
     )(core[None].astype(jnp.int32), template, voxel_maps)
 
@@ -330,28 +341,17 @@
     shard = pl.pallas_call(
         whiten_kernel,
         out_shape=jax.ShapeDtypeStruct((1, shard_rows, 128), f32),
-        grid_spec=pltpu.PrefetchScalarGridSpec(
-            num_scalar_prefetch=1,
-            grid=(1,),
-            in_specs=[
-                pl.BlockSpec((16, rows, cols), lambda i, c: (0, 0, 0)),
-                hbm,
-                hbm,
-                hbm,
-                hbm,
-                pl.BlockSpec((64, 128), lambda i, c: (0, 0)),
-            ],
-            out_specs=pl.BlockSpec((1, shard_rows, 128), lambda i, c: (0, 0, 0)),
-            scratch_shapes=[
-                pltpu.VMEM((2 * rows, length), f32),
-                pltpu.VMEM((2 * freq_pad, length), bf16),
-                pltpu.VMEM((2 * freq_pad, length), bf16),
-                pltpu.VMEM((2 * freq_pad, window), bf16),
-                pltpu.VMEM((2 * freq_pad, window), bf16),
-                pltpu.SemaphoreType.DMA((4,)),
-            ],
-        ),
-        compiler_params=pltpu.CompilerParams(vmem_limit_bytes=60 * 2**20),
+        in_specs=[smem, vmem, hbm, hbm, vmem],
+        out_specs=vmem,
+        scratch_shapes=[
+            pltpu.VMEM((2 * rows, length), f32),
+            pltpu.VMEM((2 * freq_pad, length), bf16),
+            pltpu.VMEM((2 * freq_pad, length), bf16),
+            pltpu.VMEM((2 * freq_pad, window), bf16),
+            pltpu.VMEM((2 * freq_pad, window), bf16),
+            pltpu.SemaphoreType.DMA((4,)),
+        ],
+        compiler_params=pltpu.CompilerParams(vmem_limit_bytes=52 * 2**20),
         name="whiten",
     )(column[None].astype(jnp.int32), full_rows, *tables, own)
 
@@ -361,13 +361,14 @@
     mine, theirs, scale = pl.pallas_call(
         match_kernel,
         out_shape=[jax.ShapeDtypeStruct((rows, cols), f32)] * 3,
-        in_specs=[smem, hbm, hbm],
+        in_specs=[smem, vmem, vmem],
         out_specs=[vmem] * 3,
         scratch_shapes=match_scratch(),
-        compiler_params=pltpu.CompilerParams(vmem_limit_bytes=56 * 2**20),
+        compiler_params=pltpu.CompilerParams(vmem_limit_bytes=32 * 2**20),
         name="match",
     )(place, gathered, partner)
-    received = lax.ppermute(theirs, "ylo", [(0, 1), (1, 0)])
+    both = lax.all_gather(theirs, "ylo")
+    received = lax.dynamic_index_in_dim(both, 1 - ylo, 0, keepdims=False)
     return (jnp.maximum(mine, received) * scale)[None]
 
 

time: 110 us -> 97 us (0.88)
  Pallas kernels: 39.9 us -> 30.2 us
  blocking collectives: 35.9 us -> 38.5 us
  starting transfers between devices: 20.5 us -> 18 us
  waiting for transfers between devices: 7.48 us -> 5.95 us
  other arithmetic: 2 us -> 0.69 us
    pallas_call x1, Pallas kernels: 30.4 us -> 24.3 us  [shards(): pl.pallas_call(match_kernel, out_shape=[jax.ShapeDtypeStruct((rows, cols)...]
    all_gather x0 -> x1, blocking collectives: none -> 3.27 us  [shards(): both = lax.all_gather(theirs, 'ylo')]
    ppermute x1 -> x0, starting transfers between devices: 2.42 us -> none  [shards(): received = lax.ppermute(theirs, 'ylo', [(0, 1), (1, 0)])]
    ppermute x1 -> x0, waiting for transfers between devices: 2.26 us -> none  [shards(): received = lax.ppermute(theirs, 'ylo', [(0, 1), (1, 0)])]
    pallas_call x1, Pallas kernels: 3.99 us -> 2 us  [shards(): pl.pallas_call(rotate_kernel, out_shape=jax.ShapeDtypeStruct((half_rows,...]
    pallas_call x1, Pallas kernels: 5.46 us -> 3.92 us  [shards(): pl.pallas_call(whiten_kernel, out_shape=jax.ShapeDtypeStruct((1, shard_ro...]
    ppermute x1 -> x0, local copies, waits for them, and re-layouts: 1.35 us -> none  [shards(): partner = lax.ppermute(gathered, 'core', [(0, 1), (1, 0)])]
  transfers between devices with their start and end apart: 3 -> 2, of which waited for: 3 -> 2; matrix products, arithmetic and copies ran while one was open for 1% -> 0% of each run, Pallas kernels for 4% -> 2%
where the time goes in v3:
time: 97 us; the launch traced here: 96.6 us
  blocking collectives  38.5 us (40%)
  Pallas kernels  30.2 us (31%)
  starting transfers between devices  18 us (19%)
  waiting for transfers between devices  5.95 us (6%)
  local copies, waits for them, and re-layouts  3.21 us (3%)
    all_gather x1, blocking collectives, shards(): gathered = lax.all_gather(shard, 'z', axis=0, tiled=True)  35.2 us
    pallas_call x1, Pallas kernels, shards(): pl.pallas_call(match_kernel, out_shape=[jax.ShapeDtypeStruct((rows, cols)...  24.3 us
    ppermute x1, starting transfers between devices, shards(): partner = lax.ppermute(gathered, 'core', [(0, 1), (1, 0)])  10.4 us
    all_to_all x1, starting transfers between devices, shards(): lax.all_to_all(copies, group, split_axis=0, concat_axis=0, tiled=True)  7.58 us
    pallas_call x1, Pallas kernels, shards(): pl.pallas_call(whiten_kernel, out_shape=jax.ShapeDtypeStruct((1, shard_ro...  3.92 us
    all_to_all x1, waiting for transfers between devices, shards(): lax.all_to_all(copies, group, split_axis=0, concat_axis=0, tiled=True)  3.87 us
    all_gather x1, blocking collectives, shards(): both = lax.all_gather(theirs, 'ylo')  3.27 us
    ppermute x1, waiting for transfers between devices, shards(): partner = lax.ppermute(gathered, 'core', [(0, 1), (1, 0)])  2.09 us
  transfers between devices with their start and end apart: 2, of which 2 were waited for; matrix products, arithmetic and copies ran while one was open for 0% of the time, Pallas kernels for 2%

profile of v3, /device:TPU:1, one launch (start us, length us, event | category | flops | bytes accessed | tf_op | source)
XLA Modules:
  0.0 96.6 jit_solution(12575621177870941293)
XLA Ops:
  0.0 1.4 %broadcast_in_dim.16 = f32[16,32,104]{2,1,0:T(8,128)} broadcast(f32[32,104]{1,0:T(8,128)} %bitcast.15), dimensions={1,2} | broadcast | bytes 226304 | tf_op jit(solution)/shard_map/broadcast_in_dim | solution.py:327
  1.4 7.6 %all-to-all-start = ((f32[16,32,104]{2,1,0:T(8,128)}), f32[16,32,104]{2,1,0:T(8,128)S(1)}, u32[]{:S(2)}, u32[]{:S(2)}) async-start(f32[16,32,104]{2,1,0:T(8,128)} %broadcast_in_dim.16), calls=%async_computation | async-start | bytes 524288 | tf_op jit(solution)/shard_map/all_to_all | solution.py:328
  9.0 0.0 copy-start
  9.1 1.0 copy-done
  10.0 0.0 copy-start.1
  10.0 0.8 copy-done.1
  10.8 2.0 %rotate.1.own_ref = f32[56,128]{1,0:T(8,128)S(1)} custom-call(s32[1]{0:T(128)} %bitcast.2.core_ref, f32[24,24,24]{2,1,0:T(8,128)S(1)} %copy-done, s32[1,13824]{1,0:T(1,128)S(1)} %copy-done.1), custom_call_target="tpu_custom_call" | custom-call | tf_op jit(solution)/shard_map/rotate/pallas_call | solution.py:330
  12.8 3.9 %all-to-all-done.rows_ref = f32[16,32,104]{2,1,0:T(8,128)S(1)} async-done(((f32[16,32,104]{2,1,0:T(8,128)}), f32[16,32,104]{2,1,0:T(8,128)S(1)}, u32[]{:S(2)}, u32[]{:S(2)}) %all-to-all-start) | async-done | bytes 213024 | tf_op jit(solution)/shard_map/all_to_all | solution.py:328
  16.7 3.9 %whiten.1 = f32[1,120,128]{2,1,0:T(8,128)S(1)} custom-call(s32[1]{0:T(128)} %bitcast.3.place_ref, f32[16,32,104]{2,1,0:T(8,128)S(1)} %all-to-all-done.rows_ref, bf16[2,864,832]{2,1,0:T(8,128)(2,1)} %constant.35.clone.f_hbm, bf16[2,8,864,128]{3,2,1,0:T(8,128)(2,1)} %constant.36.clone.b_hbm, f32[56,128]{1,0:T(8,128)S(1)} %rotate.1.own_ref), custom_call_target="tpu_custom_call" | custom-call | tf_op jit(solution)/shard_map/whiten/pallas_call | solution.py:341
  20.6 35.2 %all_gather.9.own_ref = f32[16,120,128]{2,1,0:T(8,128)S(1)} all-gather(f32[1,120,128]{2,1,0:T(8,128)S(1)} %whiten.1), channel_id=1, replica_groups=mesh['ylo'=2,'z'=16,'core'=2,'x'=4,'yhi'=2] {'z'}, dimensions={0}, use_global_device_ids=true | all-gather | bytes 1044480 | tf_op jit(solution)/shard_map/all_gather | solution.py:358
  55.8 10.4 %collective-permute-start = (f32[16,120,128]{2,1,0:T(8,128)S(1)}, f32[16,120,128]{2,1,0:T(8,128)S(1)}, u32[]{:S(2)}, u32[]{:S(2)}) collective-permute-start(f32[16,120,128]{2,1,0:T(8,128)S(1)} %all_gather.9.own_ref), channel_id=1, source_target_pairs={{0,8},{8,0},{1,9},{9,1},{2,10},{10,2},{3,11},{11,3},{4,12},{12,4},... | collective-permute-start | bytes 2949128 | tf_op jit(solution)/shard_map/ppermute | solution.py:359
  66.3 0.1 pad_add_fusion.where_ref
  66.4 2.1 %collective-permute-done.other_ref = f32[16,120,128]{2,1,0:T(8,128)S(1)} collective-permute-done((f32[16,120,128]{2,1,0:T(8,128)S(1)}, f32[16,120,128]{2,1,0:T(8,128)S(1)}, u32[]{:S(2)}, u32[]{:S(2)}) %collective-permute-start) | collective-permute-done | bytes 983072 | tf_op jit(solution)/shard_map/ppermute | solution.py:359
  68.5 24.3 %match.1 = (f32[32,104]{1,0:T(8,128)S(1)}, f32[32,104]{1,0:T(8,128)S(1)}, f32[32,104]{1,0:T(8,128)S(1)}) custom-call(s32[3]{0:T(128)S(1)} %pad_add_fusion.where_ref, f32[16,120,128]{2,1,0:T(8,128)S(1)} %all_gather.9.own_ref, f32[16,120,128]{2,1,0:T(8,128)S(1)} %collective-permute-done.other_ref), custom_call_target="tpu_custom_call" | custom-call | tf_op jit(solution)/shard_map/match/pallas_call | solution.py:361
  92.8 3.3 %all-gather = f32[64,104]{1,0:T(8,128)S(1)} all-gather(f32[32,104]{1,0:T(8,128)S(1)} %get-tuple-element.9), channel_id=2, replica_groups=mesh['ylo'=2,'z'=16,'core'=2,'x'=4,'yhi'=2] {'ylo'}, dimensions={0}, use_global_device_ids=true | all-gather | bytes 39936 | tf_op jit(solution)/shard_map/all_gather | solution.py:370
  96.0 0.6 fusion.1
Async XLA Ops:
  1.4 15.3 %all-to-all-start = ((f32[16,32,104]{2,1,0:T(8,128)}), f32[16,32,104]{2,1,0:T(8,128)S(1)}, u32[]{:S(2)}, u32[]{:S(2)}) async-start(f32[16,32,104]{2,1,0:T(8,128)} %broadcast_in_dim.16), calls=%async_computation | async-start | bytes 524288 | tf_op jit(solution)/shard_map/all_to_all | solution.py:328
  9.0 1.0 copy-start
  10.0 0.8 copy-start.1
  55.8 12.6 %collective-permute-start = (f32[16,120,128]{2,1,0:T(8,128)S(1)}, f32[16,120,128]{2,1,0:T(8,128)S(1)}, u32[]{:S(2)}, u32[]{:S(2)}) collective-permute-start(f32[16,120,128]{2,1,0:T(8,128)S(1)} %all_gather.9.own_ref), channel_id=1, source_target_pairs={{0,8},{8,0},{1,9},{9,1},{2,10},{10,2},{3,11},{11,3},{4,12},{12,4},... | collective-permute-start | bytes 2949128 | tf_op jit(solution)/shard_map/ppermute | solution.py:359

commit v4 on v3

--- a/solution.py
+++ b/solution.py
@@ -32,6 +32,9 @@
 depth = 32 * edge
 f32 = jnp.float32
 bf16 = jnp.bfloat16
+f8 = jnp.float8_e4m3fn
+volume_full, volume_low = 2.0**2, 2.0**11
+template_full, template_low = 2.0**8, 2.0**17
 nt = (((1,), (1,)), ((), ()))
 tn = (((0,), (0,)), ((), ()))
 
@@ -165,7 +168,7 @@
 
 
 def match_kernel(
-    where_ref, own_ref, other_ref, mine_ref, theirs_ref, scale_ref, v_ref, t_ref, l_ref, w_ref, acc_ref, best_ref, score_ref
+    where_ref, own_ref, other_ref, mine_ref, theirs_ref, scale_ref, v_ref, t_ref, l_ref, l8_ref, w_ref, w8_ref, acc_ref, acc8_ref, best_ref, score_ref, next_ref
 ):
     z0 = where_ref[0]
     ylo = where_ref[1]
@@ -187,7 +190,7 @@
         inside = jnp.logical_and(j >= 16 * ylo, j < 16 * ylo + edge).astype(f32)
         return energy + full * full * inside
 
-    energy = lax.fori_loop(0, span, load_plane, jnp.zeros((56, window), f32), unroll=4)
+    energy = lax.fori_loop(0, span, load_plane, jnp.zeros((56, window), f32), unroll=8)
 
     lane = lax.broadcasted_iota(jnp.int32, (blocks, window), 1)
     place = lax.broadcasted_iota(jnp.int32, (blocks, window), 0)
@@ -216,7 +219,7 @@
                         t_ref[r, quad, put + low : put + high, :] = total
             return carry
 
-        lax.fori_loop(0, rots, step, 0, unroll=2)
+        lax.fori_loop(0, rots, step, 0, unroll=4)
 
     @pl.when(core == 0)
     def from_first():
@@ -226,44 +229,65 @@
     def from_second():
         widen((other_ref, own_ref))
 
-    def expand(u, carry):
-        here = pl.ds(pl.multiple_of(u * blocks, blocks), blocks)
+    next_ref[...] = jnp.zeros_like(next_ref)
+
+    def expand(step, carry):
+        i = 13 - step
+        here = pl.ds(pl.multiple_of(2 * blocks * i, 2 * blocks), 2 * blocks)
         for parity in range(2):
             for quad in range(span // 4):
-                total = None
-                for part in range(4):
-                    row = jnp.broadcast_to(v_ref[4 * quad + part, pl.ds(2 * u + parity, 1), :], (blocks, window))
-                    total = row if total is None else jnp.where(owner >= part, row, total)
-                total = pltpu.roll(total, 8, 1, stride=8, stride_axis=0)
-                high, low = split(total)
-                for k, piece in enumerate((high, low, high)):
-                    at = window * (6 * quad + 3 * parity + k)
-                    l_ref[here, at : at + window] = piece
+                totals = []
+                for u in range(2):
+                    total = None
+                    for part in range(4):
+                        at = pl.ds(4 * i + 2 * u + parity, 1)
+                        row = jnp.broadcast_to(v_ref[4 * quad + part, at, :], (blocks, window))
+                        total = row if total is None else jnp.where(owner >= part, row, total)
+                    totals.append(pltpu.roll(total, 8, 1, stride=8, stride_axis=0))
+                totals.append(next_ref[parity, quad])
+                next_ref[parity, quad] = totals[0]
+                for tap in (parity, 2 + parity):
+                    values = jnp.concatenate(totals[tap // 2 : tap // 2 + 2], axis=0)
+                    high = values.astype(bf16)
+                    low = ((values - high.astype(f32)) * volume_low).astype(f8)
+                    full = (values * volume_full).astype(f8)
+                    cell16 = window * (4 * quad + tap)
+                    l_ref[here, cell16 : cell16 + window] = high
+                    l8_ref[here, 2 * cell16 : 2 * cell16 + window] = low
+                    l8_ref[here, 2 * cell16 + window : 2 * cell16 + 2 * window] = full
         return carry
 
-    lax.fori_loop(0, 28, expand, 0, unroll=4)
-
-    def build(v, slot):
-        for tap, targets in ((-1, ((0, 1),)), (0, ((0, 0), (1, 1))), (1, ((1, 0),))):
-            for pair in range(rots // 2):
+    lax.fori_loop(0, 14, expand, 0, unroll=2)
+
+    def build(i, slot):
+        for tap in range(-1, 4):
+            targets = [(tap, 0)] * (tap >= 0) + [(tap + 1, 1)] * (tap < 3)
+            for four in range(rots // 4):
                 for quad in range(6):
                     moved = []
-                    for r in (2 * pair, 2 * pair + 1):
-                        row = t_ref[r, quad, pl.ds(2 * v + tap + 1, 1), :]
+                    for r in range(4 * four, 4 * four + 4):
+                        row = t_ref[r, quad, pl.ds(4 * i + tap + 1, 1), :]
                         moved.append(pltpu.roll(jnp.broadcast_to(row, (8, window)), 0, 1, stride=1, stride_axis=0))
-                    high, low = split(jnp.concatenate(moved, axis=0))
-                    for parity, p in targets:
-                        for k, piece in enumerate((high, high, low)):
-                            at = window * (6 * quad + 3 * parity + k)
-                            place = 128 * p + 16 * pair
-                            w_ref[slot, place : place + 16, at : at + window] = piece
-
-    def product(v, slot):
-        here = pl.ds(pl.multiple_of(v * blocks, blocks), 16 * blocks)
-        left = jnp.concatenate([l_ref[here, : 6 * depth], l_ref[here, 4 * depth : 10 * depth]], axis=0)
+                    values = jnp.concatenate(moved, axis=0)
+                    high = values.astype(bf16)
+                    low = ((values - high.astype(f32)) * template_low).astype(f8)
+                    full = (values * template_full).astype(f8)
+                    for t, p in targets:
+                        cell16 = window * (4 * quad + t)
+                        at = slice(128 * p + 32 * four, 128 * p + 32 * (four + 1))
+                        w_ref[slot, at, cell16 : cell16 + window] = high
+                        w8_ref[slot, at, 2 * cell16 : 2 * cell16 + window] = full
+                        w8_ref[slot, at, 2 * cell16 + window : 2 * cell16 + 2 * window] = low
+
+    def product(i, slot):
+        here = pl.ds(pl.multiple_of(2 * i * blocks, 2 * blocks), 16 * blocks)
+        left = jnp.concatenate([l_ref[here, : 24 * window], l_ref[here, 16 * window :]], axis=0)
         acc_ref[...] += lax.dot_general(left, w_ref[slot], nt, preferred_element_type=f32)
+        left = jnp.concatenate([l8_ref[here, : 48 * window], l8_ref[here, 32 * window :]], axis=0)
+        acc8_ref[...] += lax.dot_general(left, w8_ref[slot], nt, preferred_element_type=f32)
 
     acc_ref[...] = jnp.zeros_like(acc_ref)
+    acc8_ref[...] = jnp.zeros_like(acc8_ref)
     build(0, 0)
 
     def step(i, carry):
@@ -273,12 +297,13 @@
         product(2 * i + 1, 1)
         return carry
 
-    lax.fori_loop(0, 6, step, 0)
-    product(12, 0)
+    lax.fori_loop(0, 3, step, 0)
+    product(6, 0)
 
     lanes = lax.broadcasted_iota(jnp.int32, (16, window), 1)
     for p in range(2):
-        best = acc_ref[:, 128 * p : 128 * (p + 1)]
+        at = slice(128 * p, 128 * (p + 1))
+        best = acc_ref[:, at] + acc8_ref[:, at] * (1.0 / (volume_low * template_full))
         for shift in (64, 32, 16, 8):
             best = jnp.maximum(best, pltpu.roll(best, shift, 1))
         best_ref[...] = best
@@ -309,11 +334,15 @@
     return [
         pltpu.VMEM((span, 56, window), f32),
         pltpu.VMEM((rots, 6, 32, window), f32),
-        pltpu.VMEM((28 * blocks, 10 * depth), bf16),
-        pltpu.VMEM((2, 256, 6 * depth), bf16),
+        pltpu.VMEM((28 * blocks, 40 * window), bf16),
+        pltpu.VMEM((28 * blocks, 80 * window), f8),
+        pltpu.VMEM((2, 256, 24 * window), bf16),
+        pltpu.VMEM((2, 256, 48 * window), f8),
+        pltpu.VMEM((32 * blocks, 256), f32),
         pltpu.VMEM((32 * blocks, 256), f32),
         pltpu.VMEM((32 * blocks, 128), f32),
         pltpu.VMEM((2 * rows, 128), f32),
+        pltpu.VMEM((2, span // 4, blocks, window), f32),
     ]
 
 

time: 97 us -> 91.7 us (0.945)
  Pallas kernels: 30.2 us -> 25 us
    pallas_call x1, Pallas kernels: 24.3 us -> 19 us  [shards(): pl.pallas_call(match_kernel, out_shape=[jax.ShapeDtypeStruct((rows, cols)...]
where the time goes in v4:
time: 91.7 us; the launch traced here: 91.4 us
  blocking collectives  38.5 us (42%)
  Pallas kernels  25 us (27%)
  starting transfers between devices  18 us (20%)
  waiting for transfers between devices  5.95 us (6%)
  local copies, waits for them, and re-layouts  3.21 us (4%)
    all_gather x1, blocking collectives, shards(): gathered = lax.all_gather(shard, 'z', axis=0, tiled=True)  35.2 us
    pallas_call x1, Pallas kernels, shards(): pl.pallas_call(match_kernel, out_shape=[jax.ShapeDtypeStruct((rows, cols)...  19 us
    ppermute x1, starting transfers between devices, shards(): partner = lax.ppermute(gathered, 'core', [(0, 1), (1, 0)])  10.4 us
    all_to_all x1, starting transfers between devices, shards(): lax.all_to_all(copies, group, split_axis=0, concat_axis=0, tiled=True)  7.58 us
    pallas_call x1, Pallas kernels, shards(): pl.pallas_call(whiten_kernel, out_shape=jax.ShapeDtypeStruct((1, shard_ro...  3.92 us
    all_to_all x1, waiting for transfers between devices, shards(): lax.all_to_all(copies, group, split_axis=0, concat_axis=0, tiled=True)  3.87 us
    all_gather x1, blocking collectives, shards(): both = lax.all_gather(theirs, 'ylo')  3.27 us
    ppermute x1, waiting for transfers between devices, shards(): partner = lax.ppermute(gathered, 'core', [(0, 1), (1, 0)])  2.09 us
  transfers between devices with their start and end apart: 2, of which 2 were waited for; matrix products, arithmetic and copies ran while one was open for 0% of the time, Pallas kernels for 2%

profile of v4, /device:TPU:1, one launch (start us, length us, event | category | flops | bytes accessed | tf_op | source)
XLA Modules:
  0.0 91.4 jit_solution(9018627008527244333)
XLA Ops:
  0.0 1.4 %broadcast_in_dim.16 = f32[16,32,104]{2,1,0:T(8,128)} broadcast(f32[32,104]{1,0:T(8,128)} %bitcast.15), dimensions={1,2} | broadcast | bytes 226304 | tf_op jit(solution)/shard_map/broadcast_in_dim | solution.py:356
  1.4 7.6 %all-to-all-start = ((f32[16,32,104]{2,1,0:T(8,128)}), f32[16,32,104]{2,1,0:T(8,128)S(1)}, u32[]{:S(2)}, u32[]{:S(2)}) async-start(f32[16,32,104]{2,1,0:T(8,128)} %broadcast_in_dim.16), calls=%async_computation | async-start | bytes 524288 | tf_op jit(solution)/shard_map/all_to_all | solution.py:357
  9.0 0.0 copy-start
  9.1 1.0 %copy-done = f32[24,24,24]{2,1,0:T(8,128)S(1)} copy-done((f32[24,24,24]{2,1,0:T(8,128)S(1)}, f32[24,24,24]{2,1,0:T(8,128)}, u32[]{:S(2)}) %copy-start) | copy-done | bytes 55320
  10.0 0.0 copy-start.1
  10.0 0.8 copy-done.1
  10.8 2.0 %rotate.1.own_ref = f32[56,128]{1,0:T(8,128)S(1)} custom-call(s32[1]{0:T(128)} %bitcast.2.core_ref, f32[24,24,24]{2,1,0:T(8,128)S(1)} %copy-done, s32[1,13824]{1,0:T(1,128)S(1)} %copy-done.1), custom_call_target="tpu_custom_call" | custom-call | tf_op jit(solution)/shard_map/rotate/pallas_call | solution.py:359
  12.8 3.9 %all-to-all-done.rows_ref = f32[16,32,104]{2,1,0:T(8,128)S(1)} async-done(((f32[16,32,104]{2,1,0:T(8,128)}), f32[16,32,104]{2,1,0:T(8,128)S(1)}, u32[]{:S(2)}, u32[]{:S(2)}) %all-to-all-start) | async-done | bytes 213024 | tf_op jit(solution)/shard_map/all_to_all | solution.py:357
  16.7 3.9 %whiten.1 = f32[1,120,128]{2,1,0:T(8,128)S(1)} custom-call(s32[1]{0:T(128)} %bitcast.3.place_ref, f32[16,32,104]{2,1,0:T(8,128)S(1)} %all-to-all-done.rows_ref, bf16[2,864,832]{2,1,0:T(8,128)(2,1)} %constant.35.clone.f_hbm, bf16[2,8,864,128]{3,2,1,0:T(8,128)(2,1)} %constant.36.clone.b_hbm, f32[56,128]{1,0:T(8,128)S(1)} %rotate.1.own_ref), custom_call_target="tpu_custom_call" | custom-call | tf_op jit(solution)/shard_map/whiten/pallas_call | solution.py:370
  20.6 35.2 %all_gather.9.own_ref = f32[16,120,128]{2,1,0:T(8,128)S(1)} all-gather(f32[1,120,128]{2,1,0:T(8,128)S(1)} %whiten.1), channel_id=1, replica_groups=mesh['ylo'=2,'z'=16,'core'=2,'x'=4,'yhi'=2] {'z'}, dimensions={0}, use_global_device_ids=true | all-gather | bytes 1044480 | tf_op jit(solution)/shard_map/all_gather | solution.py:387
  55.8 10.4 %collective-permute-start = (f32[16,120,128]{2,1,0:T(8,128)S(1)}, f32[16,120,128]{2,1,0:T(8,128)S(1)}, u32[]{:S(2)}, u32[]{:S(2)}) collective-permute-start(f32[16,120,128]{2,1,0:T(8,128)S(1)} %all_gather.9.own_ref), channel_id=1, source_target_pairs={{0,8},{8,0},{1,9},{9,1},{2,10},{10,2},{3,11},{11,3},{4,12},{12,4},... | collective-permute-start | bytes 2949128 | tf_op jit(solution)/shard_map/ppermute | solution.py:388
  66.3 0.1 pad_add_fusion.where_ref
  66.4 2.1 %collective-permute-done.other_ref = f32[16,120,128]{2,1,0:T(8,128)S(1)} collective-permute-done((f32[16,120,128]{2,1,0:T(8,128)S(1)}, f32[16,120,128]{2,1,0:T(8,128)S(1)}, u32[]{:S(2)}, u32[]{:S(2)}) %collective-permute-start) | collective-permute-done | bytes 983072 | tf_op jit(solution)/shard_map/ppermute | solution.py:388
  68.5 19.0 %match.1 = (f32[32,104]{1,0:T(8,128)S(1)}, f32[32,104]{1,0:T(8,128)S(1)}, f32[32,104]{1,0:T(8,128)S(1)}) custom-call(s32[3]{0:T(128)S(1)} %pad_add_fusion.where_ref, f32[16,120,128]{2,1,0:T(8,128)S(1)} %all_gather.9.own_ref, f32[16,120,128]{2,1,0:T(8,128)S(1)} %collective-permute-done.other_ref), custom_call_target="tpu_custom_call" | custom-call | tf_op jit(solution)/shard_map/match/pallas_call | solution.py:390
  87.5 3.3 %all-gather = f32[64,104]{1,0:T(8,128)S(1)} all-gather(f32[32,104]{1,0:T(8,128)S(1)} %get-tuple-element.9), channel_id=2, replica_groups=mesh['ylo'=2,'z'=16,'core'=2,'x'=4,'yhi'=2] {'ylo'}, dimensions={0}, use_global_device_ids=true | all-gather | bytes 39936 | tf_op jit(solution)/shard_map/all_gather | solution.py:399
  90.8 0.6 fusion.1
Async XLA Ops:
  1.4 15.3 %all-to-all-start = ((f32[16,32,104]{2,1,0:T(8,128)}), f32[16,32,104]{2,1,0:T(8,128)S(1)}, u32[]{:S(2)}, u32[]{:S(2)}) async-start(f32[16,32,104]{2,1,0:T(8,128)} %broadcast_in_dim.16), calls=%async_computation | async-start | bytes 524288 | tf_op jit(solution)/shard_map/all_to_all | solution.py:357
  9.0 1.0 %copy-start = (f32[24,24,24]{2,1,0:T(8,128)S(1)}, f32[24,24,24]{2,1,0:T(8,128)}, u32[]{:S(2)}) copy-start(f32[24,24,24]{2,1,0:T(8,128)} %template_ref.1) | copy-start | bytes 165892
  10.0 0.8 copy-start.1
  55.8 12.6 %collective-permute-start = (f32[16,120,128]{2,1,0:T(8,128)S(1)}, f32[16,120,128]{2,1,0:T(8,128)S(1)}, u32[]{:S(2)}, u32[]{:S(2)}) collective-permute-start(f32[16,120,128]{2,1,0:T(8,128)S(1)} %all_gather.9.own_ref), channel_id=1, source_target_pairs={{0,8},{8,0},{1,9},{9,1},{2,10},{10,2},{3,11},{11,3},{4,12},{12,4},... | collective-permute-start | bytes 2949128 | tf_op jit(solution)/shard_map/ppermute | solution.py:388

commit v5 on v4

--- a/solution.py
+++ b/solution.py
@@ -79,7 +79,9 @@
     return [(half * j + b - 4 * (a - 22), 120, 8 * j, 8) for j in range(3)]
 
 
-def rotate_kernel(core_ref, template_ref, map_ref, out_ref, normed_ref, index_ref):
+def rotate_kernel(core_ref, template_ref, map_ref, f_hbm, out_ref, f_ref, normed_ref, index_ref, sem):
+    copy = pltpu.make_async_copy(f_hbm, f_ref, sem)
+    copy.start()
     values = template_ref[...]
     centred = values - jnp.sum(values) / voxels
     normed = centred / jnp.sqrt(jnp.sum(centred * centred) + epsilon)
@@ -121,17 +123,14 @@
         return carry
 
     lax.fori_loop(0, half_rows // 8, gather, 0, unroll=7)
-
-
-def whiten_kernel(
-    place_ref, rows_ref, f_hbm, b_hbm, own_ref, out_ref, x_ref, fh_ref, fl_ref, bh_ref, bl_ref, sems
-):
+    copy.wait()
+
+
+def whiten_kernel(place_ref, rows_ref, f_ref, b_hbm, own_ref, out_ref, x_ref, bh_ref, bl_ref, sems):
     column = place_ref[0]
     copies = [
-        pltpu.make_async_copy(f_hbm.at[0], fh_ref, sems.at[0]),
-        pltpu.make_async_copy(f_hbm.at[1], fl_ref, sems.at[1]),
-        pltpu.make_async_copy(b_hbm.at[0, column], bh_ref, sems.at[2]),
-        pltpu.make_async_copy(b_hbm.at[1, column], bl_ref, sems.at[3]),
+        pltpu.make_async_copy(b_hbm.at[0, column], bh_ref, sems.at[0]),
+        pltpu.make_async_copy(b_hbm.at[1, column], bl_ref, sems.at[1]),
     ]
     for copy in copies:
         copy.start()
@@ -142,12 +141,11 @@
                 plane * 8 + j
             ]
     xh, xl = split(x_ref[...])
-    copies[0].wait()
-    spec = lax.dot_general(fh_ref[...], xh, nt, preferred_element_type=f32) + lax.dot_general(
-        fh_ref[...], xl, nt, preferred_element_type=f32
+    spec = (
+        lax.dot_general(f_ref[0], xh, nt, preferred_element_type=f32)
+        + lax.dot_general(f_ref[0], xl, nt, preferred_element_type=f32)
+        + lax.dot_general(f_ref[1], xh, nt, preferred_element_type=f32)
     )
-    copies[1].wait()
-    spec = spec + lax.dot_general(fl_ref[...], xh, nt, preferred_element_type=f32)
     real = spec[:freq_pad]
     imag = spec[freq_pad:]
     power = real * real + imag * imag
@@ -158,8 +156,8 @@
     smoothed = (before + power + after) / 3.0 + floor_share * (total / length) + epsilon
     weights = lax.rsqrt(smoothed)
     wh, wl = split(jnp.concatenate([real * weights, imag * weights], axis=0))
-    copies[2].wait()
-    copies[3].wait()
+    copies[0].wait()
+    copies[1].wait()
     out_ref[0, : 2 * rows, :] = (
         lax.dot_general(wh, bh_ref[...], tn, preferred_element_type=f32)
         + lax.dot_general(wl, bh_ref[...], tn, preferred_element_type=f32)
@@ -185,8 +183,9 @@
         v_ref[j, half : half + rows, :] = own_ref[z, pl.ds(start, rows), :] * valid
         v_ref[j, 0:half, :] = near[rows - half :] * (valid * (1.0 - first))
         v_ref[j, half + rows : 56, :] = near[:half] * (valid * first)
-        full = v_ref[j]
-        v_ref[j] = pltpu.roll(full, (j % 4) * 32, 1)
+        v_ref[j, 56:, :] = jnp.zeros((8, window), f32)
+        full = v_ref[j, :56, :]
+        v_ref[j, :56, :] = pltpu.roll(full, (j % 4) * 32, 1)
         inside = jnp.logical_and(j >= 16 * ylo, j < 16 * ylo + edge).astype(f32)
         return energy + full * full * inside
 
@@ -199,53 +198,44 @@
 
     t_ref[...] = jnp.zeros_like(t_ref)
 
-    def widen(sources):
-        def placed(total, source, lane_from, lane_to, width):
-            moved = pltpu.roll(source, (lane_to - lane_from) % window, 1)
-            at = cell[: source.shape[0]]
-            return jnp.where(jnp.logical_and(at >= lane_to, at < lane_to + width), moved, total)
-
-        def step(r, carry):
-            for k, source_ref in enumerate(sources):
-                put = 1 + half * k
-                for quad in range(6):
-                    for low, high in ((0, 8), (8, half)) if quad == 5 else ((0, half),):
-                        total = jnp.zeros((high - low, window), f32)
-                        for part in range(4):
-                            for at, lane_from, c, width in cells_of(4 * quad + part, low):
-                                at = 2 * rows + at
-                                source = source_ref[r, at : at + high - low, :]
-                                total = placed(total, source, lane_from, 32 * part + c, width)
-                        t_ref[r, quad, put + low : put + high, :] = total
-            return carry
-
-        lax.fori_loop(0, rots, step, 0, unroll=4)
-
-    @pl.when(core == 0)
-    def from_first():
-        widen((own_ref, other_ref))
-
-    @pl.when(core != 0)
-    def from_second():
-        widen((other_ref, own_ref))
-
-    next_ref[...] = jnp.zeros_like(next_ref)
-
-    def expand(step, carry):
-        i = 13 - step
-        here = pl.ds(pl.multiple_of(2 * blocks * i, 2 * blocks), 2 * blocks)
+    def placed(total, source, lane_from, lane_to, width):
+        moved = pltpu.roll(source, (lane_to - lane_from) % window, 1)
+        at = cell[: source.shape[0]]
+        return jnp.where(jnp.logical_and(at >= lane_to, at < lane_to + width), moved, total)
+
+    def widen(k, r):
+        mine = core == k
+        put = 1 + half * k
+        for quad in range(6):
+            for low, high in ((0, 8), (8, half)) if quad == 5 else ((0, half),):
+                total = jnp.zeros((high - low, window), f32)
+                for part in range(4):
+                    for at, lane_from, c, width in cells_of(4 * quad + part, low):
+                        at = slice(2 * rows + at, 2 * rows + at + high - low)
+                        source = jnp.where(mine, own_ref[r, at, :], other_ref[r, at, :])
+                        total = placed(total, source, lane_from, 32 * part + c, width)
+                t_ref[r, quad, put + low : put + high, :] = total
+
+    def widen_first(r, carry):
+        widen(0, r)
+        return carry
+
+    lax.fori_loop(0, rots, widen_first, 0, unroll=4)
+
+    def total_of(u, parity, quad):
+        total = None
+        for part in range(4):
+            row = jnp.broadcast_to(v_ref[4 * quad + part, pl.ds(2 * u + parity, 1), :], (blocks, window))
+            total = row if total is None else jnp.where(owner >= part, row, total)
+        return pltpu.roll(total, 8, 1, stride=8, stride_axis=0)
+
+    def expand(i):
+        start = 2 * blocks * i
+        here = pl.ds(start if isinstance(i, int) else pl.multiple_of(start, 2 * blocks), 2 * blocks)
         for parity in range(2):
             for quad in range(span // 4):
-                totals = []
-                for u in range(2):
-                    total = None
-                    for part in range(4):
-                        at = pl.ds(4 * i + 2 * u + parity, 1)
-                        row = jnp.broadcast_to(v_ref[4 * quad + part, at, :], (blocks, window))
-                        total = row if total is None else jnp.where(owner >= part, row, total)
-                    totals.append(pltpu.roll(total, 8, 1, stride=8, stride_axis=0))
-                totals.append(next_ref[parity, quad])
-                next_ref[parity, quad] = totals[0]
+                totals = [next_ref[parity, quad], total_of(2 * i + 1, parity, quad), total_of(2 * i + 2, parity, quad)]
+                next_ref[parity, quad] = totals[2]
                 for tap in (parity, 2 + parity):
                     values = jnp.concatenate(totals[tap // 2 : tap // 2 + 2], axis=0)
                     high = values.astype(bf16)
@@ -255,9 +245,16 @@
                     l_ref[here, cell16 : cell16 + window] = high
                     l8_ref[here, 2 * cell16 : 2 * cell16 + window] = low
                     l8_ref[here, 2 * cell16 + window : 2 * cell16 + 2 * window] = full
+
+    for parity in range(2):
+        for quad in range(span // 4):
+            next_ref[parity, quad] = total_of(0, parity, quad)
+
+    def expand_first(i, carry):
+        expand(i)
         return carry
 
-    lax.fori_loop(0, 14, expand, 0, unroll=2)
+    lax.fori_loop(0, 8, expand_first, 0, unroll=2)
 
     def build(i, slot):
         for tap in range(-1, 4):
@@ -266,7 +263,7 @@
                 for quad in range(6):
                     moved = []
                     for r in range(4 * four, 4 * four + 4):
-                        row = t_ref[r, quad, pl.ds(4 * i + tap + 1, 1), :]
+                        row = t_ref[r, quad, 4 * i + tap + 1 : 4 * i + tap + 2, :]
                         moved.append(pltpu.roll(jnp.broadcast_to(row, (8, window)), 0, 1, stride=1, stride_axis=0))
                     values = jnp.concatenate(moved, axis=0)
                     high = values.astype(bf16)
@@ -280,7 +277,7 @@
                         w8_ref[slot, at, 2 * cell16 + window : 2 * cell16 + 2 * window] = low
 
     def product(i, slot):
-        here = pl.ds(pl.multiple_of(2 * i * blocks, 2 * blocks), 16 * blocks)
+        here = slice(2 * i * blocks, (2 * i + 16) * blocks)
         left = jnp.concatenate([l_ref[here, : 24 * window], l_ref[here, 16 * window :]], axis=0)
         acc_ref[...] += lax.dot_general(left, w_ref[slot], nt, preferred_element_type=f32)
         left = jnp.concatenate([l8_ref[here, : 48 * window], l8_ref[here, 32 * window :]], axis=0)
@@ -289,16 +286,14 @@
     acc_ref[...] = jnp.zeros_like(acc_ref)
     acc8_ref[...] = jnp.zeros_like(acc8_ref)
     build(0, 0)
-
-    def step(i, carry):
-        build(2 * i + 1, 1)
-        product(2 * i, 0)
-        build(2 * i + 2, 0)
-        product(2 * i + 1, 1)
-        return carry
-
-    lax.fori_loop(0, 3, step, 0)
-    product(6, 0)
+    for i in range(7):
+        if i < 2:
+            for r in range(8 * i, 8 * i + 8):
+                widen(1, r)
+        if i < 6:
+            build(i + 1, (i + 1) % 2)
+            expand(8 + i)
+        product(i, i % 2)
 
     lanes = lax.broadcasted_iota(jnp.int32, (16, window), 1)
     for p in range(2):
@@ -332,7 +327,7 @@
 
 def match_scratch():
     return [
-        pltpu.VMEM((span, 56, window), f32),
+        pltpu.VMEM((span, 64, window), f32),
         pltpu.VMEM((rots, 6, 32, window), f32),
         pltpu.VMEM((28 * blocks, 40 * window), bf16),
         pltpu.VMEM((28 * blocks, 80 * window), f8),
@@ -356,33 +351,37 @@
     copies = jnp.broadcast_to(volume, (16, rows, cols))
     full_rows = lax.all_to_all(copies, group, split_axis=0, concat_axis=0, tiled=True)
 
-    own = pl.pallas_call(
+    forward, backward = (jnp.asarray(table) for table in dft_tables())
+    own, forward = pl.pallas_call(
         rotate_kernel,
-        out_shape=jax.ShapeDtypeStruct((half_rows, 128), f32),
-        in_specs=[smem, vmem, vmem],
-        out_specs=vmem,
-        scratch_shapes=[pltpu.VMEM((5 * edge, 128), f32), pltpu.VMEM((half_rows, 128), jnp.int32)],
-        compiler_params=pltpu.CompilerParams(vmem_limit_bytes=8 * 2**20),
+        out_shape=[
+            jax.ShapeDtypeStruct((half_rows, 128), f32),
+            jax.ShapeDtypeStruct((2, 2 * freq_pad, length), bf16),
+        ],
+        in_specs=[smem, vmem, vmem, hbm],
+        out_specs=[vmem] * 2,
+        scratch_shapes=[
+            pltpu.VMEM((5 * edge, 128), f32),
+            pltpu.VMEM((half_rows, 128), jnp.int32),
+            pltpu.SemaphoreType.DMA,
+        ],
+        compiler_params=pltpu.CompilerParams(vmem_limit_bytes=48 * 2**20),
         name="rotate",
-    )(core[None].astype(jnp.int32), template, voxel_maps)
-
-    tables = [jnp.asarray(table) for table in dft_tables()]
+    )(core[None].astype(jnp.int32), template, voxel_maps, forward)
     shard = pl.pallas_call(
         whiten_kernel,
         out_shape=jax.ShapeDtypeStruct((1, shard_rows, 128), f32),
-        in_specs=[smem, vmem, hbm, hbm, vmem],
+        in_specs=[smem, vmem, vmem, hbm, vmem],
         out_specs=vmem,
         scratch_shapes=[
             pltpu.VMEM((2 * rows, length), f32),
-            pltpu.VMEM((2 * freq_pad, length), bf16),
-            pltpu.VMEM((2 * freq_pad, length), bf16),
             pltpu.VMEM((2 * freq_pad, window), bf16),
             pltpu.VMEM((2 * freq_pad, window), bf16),
-            pltpu.SemaphoreType.DMA((4,)),
+            pltpu.SemaphoreType.DMA((2,)),
         ],
-        compiler_params=pltpu.CompilerParams(vmem_limit_bytes=52 * 2**20),
+        compiler_params=pltpu.CompilerParams(vmem_limit_bytes=50 * 2**20),
         name="whiten",
-    )(column[None].astype(jnp.int32), full_rows, *tables, own)
+    )(column[None].astype(jnp.int32), full_rows, forward, backward, own)
 
     gathered = lax.all_gather(shard, "z", axis=0, tiled=True)
     partner = lax.ppermute(gathered, "core", [(0, 1), (1, 0)])

time: 91.7 us -> 87.4 us (0.953)
  Pallas kernels: 25 us -> 20.7 us
    pallas_call x1, Pallas kernels: 19 us -> 16.6 us  [shards(): pl.pallas_call(match_kernel, out_shape=[jax.ShapeDtypeStruct((rows, cols)...]
    pallas_call x1, Pallas kernels: 3.92 us -> 2.06 us  [shards(): pl.pallas_call(whiten_kernel, out_shape=jax.ShapeDtypeStruct((1, shard_ro...]
where the time goes in v5:
time: 87.4 us; the launch traced here: 87.1 us
  blocking collectives  38.5 us (44%)
  Pallas kernels  20.7 us (24%)
  starting transfers between devices  18 us (21%)
  waiting for transfers between devices  5.93 us (7%)
  local copies, waits for them, and re-layouts  3.21 us (4%)
    all_gather x1, blocking collectives, shards(): gathered = lax.all_gather(shard, 'z', axis=0, tiled=True)  35.2 us
    pallas_call x1, Pallas kernels, shards(): pl.pallas_call(match_kernel, out_shape=[jax.ShapeDtypeStruct((rows, cols)...  16.6 us
    ppermute x1, starting transfers between devices, shards(): partner = lax.ppermute(gathered, 'core', [(0, 1), (1, 0)])  10.4 us
    all_to_all x1, starting transfers between devices, shards(): lax.all_to_all(copies, group, split_axis=0, concat_axis=0, tiled=True)  7.58 us
    all_to_all x1, waiting for transfers between devices, shards(): lax.all_to_all(copies, group, split_axis=0, concat_axis=0, tiled=True)  3.85 us
    all_gather x1, blocking collectives, shards(): both = lax.all_gather(theirs, 'ylo')  3.27 us
    ppermute x1, waiting for transfers between devices, shards(): partner = lax.ppermute(gathered, 'core', [(0, 1), (1, 0)])  2.09 us
    pallas_call x1, Pallas kernels, shards(): pl.pallas_call(whiten_kernel, out_shape=jax.ShapeDtypeStruct((1, shard_ro...  2.06 us
  transfers between devices with their start and end apart: 2, of which 2 were waited for; matrix products, arithmetic and copies ran while one was open for 0% of the time, Pallas kernels for 2%

profile of v5, /device:TPU:1, one launch (start us, length us, event | category | flops | bytes accessed | tf_op | source)
XLA Modules:
  0.0 87.1 jit_solution(7999718538895745976)
XLA Ops:
  0.0 1.4 %broadcast_in_dim.16 = f32[16,32,104]{2,1,0:T(8,128)} broadcast(f32[32,104]{1,0:T(8,128)} %bitcast.15), dimensions={1,2} | broadcast | bytes 226304 | tf_op jit(solution)/shard_map/broadcast_in_dim | solution.py:351
  1.4 7.6 %all-to-all-start = ((f32[16,32,104]{2,1,0:T(8,128)}), f32[16,32,104]{2,1,0:T(8,128)S(1)}, u32[]{:S(2)}, u32[]{:S(2)}) async-start(f32[16,32,104]{2,1,0:T(8,128)} %broadcast_in_dim.16), calls=%async_computation | async-start | bytes 524288 | tf_op jit(solution)/shard_map/all_to_all | solution.py:352
  9.0 0.0 copy-start
  9.1 1.0 %copy-done = f32[24,24,24]{2,1,0:T(8,128)S(1)} copy-done((f32[24,24,24]{2,1,0:T(8,128)S(1)}, f32[24,24,24]{2,1,0:T(8,128)}, u32[]{:S(2)}) %copy-start) | copy-done | bytes 55320
  10.0 0.0 copy-start.1
  10.0 0.8 copy-done.1
  10.8 2.0 %rotate.1 = (f32[56,128]{1,0:T(8,128)S(1)}, bf16[2,864,832]{2,1,0:T(8,128)(2,1)S(1)}) custom-call(s32[1]{0:T(128)} %bitcast.2.core_ref, f32[24,24,24]{2,1,0:T(8,128)S(1)} %copy-done, s32[1,13824]{1,0:T(1,128)S(1)} %copy-done.1, bf16[2,864,832]{2,1,0:T(8,128)(2,1)} %constant.35.clone.f_hbm), custom_call_target="tpu_custom_call" | custom-call | tf_op jit(solution)/shard_map/rotate/pallas_call | solution.py:355
  12.8 3.8 %all-to-all-done.rows_ref = f32[16,32,104]{2,1,0:T(8,128)S(1)} async-done(((f32[16,32,104]{2,1,0:T(8,128)}), f32[16,32,104]{2,1,0:T(8,128)S(1)}, u32[]{:S(2)}, u32[]{:S(2)}) %all-to-all-start) | async-done | bytes 213024 | tf_op jit(solution)/shard_map/all_to_all | solution.py:352
  16.7 2.1 %whiten.1 = f32[1,120,128]{2,1,0:T(8,128)S(1)} custom-call(s32[1]{0:T(128)} %bitcast.3.place_ref, f32[16,32,104]{2,1,0:T(8,128)S(1)} %all-to-all-done.rows_ref, bf16[2,864,832]{2,1,0:T(8,128)(2,1)S(1)} %get-tuple-element.10.f_ref, bf16[2,8,864,128]{3,2,1,0:T(8,128)(2,1)} %constant.36.clone.b_hbm, f32[56,128]{1,0:T(8,128)S(1)} %get-tuple-element.11.own_ref), custom_call_target="tpu_custom_call" | custom-call | tf_op jit(solution)/shard_map/whiten/pallas_call | solution.py:371
  18.8 35.2 %all_gather.9.own_ref = f32[16,120,128]{2,1,0:T(8,128)S(1)} all-gather(f32[1,120,128]{2,1,0:T(8,128)S(1)} %whiten.1), channel_id=1, replica_groups=mesh['ylo'=2,'z'=16,'core'=2,'x'=4,'yhi'=2] {'z'}, dimensions={0}, use_global_device_ids=true | all-gather | bytes 1044480 | tf_op jit(solution)/shard_map/all_gather | solution.py:386
  54.0 10.4 %collective-permute-start = (f32[16,120,128]{2,1,0:T(8,128)S(1)}, f32[16,120,128]{2,1,0:T(8,128)S(1)}, u32[]{:S(2)}, u32[]{:S(2)}) collective-permute-start(f32[16,120,128]{2,1,0:T(8,128)S(1)} %all_gather.9.own_ref), channel_id=1, source_target_pairs={{0,8},{8,0},{1,9},{9,1},{2,10},{10,2},{3,11},{11,3},{4,12},{12,4},... | collective-permute-start | bytes 2949128 | tf_op jit(solution)/shard_map/ppermute | solution.py:387
  64.4 0.1 pad_add_fusion.where_ref
  64.5 2.1 %collective-permute-done.other_ref = f32[16,120,128]{2,1,0:T(8,128)S(1)} collective-permute-done((f32[16,120,128]{2,1,0:T(8,128)S(1)}, f32[16,120,128]{2,1,0:T(8,128)S(1)}, u32[]{:S(2)}, u32[]{:S(2)}) %collective-permute-start) | collective-permute-done | bytes 983072 | tf_op jit(solution)/shard_map/ppermute | solution.py:387
  66.6 16.6 %match.1 = (f32[32,104]{1,0:T(8,128)S(1)}, f32[32,104]{1,0:T(8,128)S(1)}, f32[32,104]{1,0:T(8,128)S(1)}) custom-call(s32[3]{0:T(128)S(1)} %pad_add_fusion.where_ref, f32[16,120,128]{2,1,0:T(8,128)S(1)} %all_gather.9.own_ref, f32[16,120,128]{2,1,0:T(8,128)S(1)} %collective-permute-done.other_ref), custom_call_target="tpu_custom_call" | custom-call | tf_op jit(solution)/shard_map/match/pallas_call | solution.py:389
  83.2 3.3 %all-gather = f32[64,104]{1,0:T(8,128)S(1)} all-gather(f32[32,104]{1,0:T(8,128)S(1)} %get-tuple-element.13), channel_id=2, replica_groups=mesh['ylo'=2,'z'=16,'core'=2,'x'=4,'yhi'=2] {'ylo'}, dimensions={0}, use_global_device_ids=true | all-gather | bytes 39936 | tf_op jit(solution)/shard_map/all_gather | solution.py:398
  86.5 0.6 fusion.1
Async XLA Ops:
  1.4 15.3 %all-to-all-start = ((f32[16,32,104]{2,1,0:T(8,128)}), f32[16,32,104]{2,1,0:T(8,128)S(1)}, u32[]{:S(2)}, u32[]{:S(2)}) async-start(f32[16,32,104]{2,1,0:T(8,128)} %broadcast_in_dim.16), calls=%async_computation | async-start | bytes 524288 | tf_op jit(solution)/shard_map/all_to_all | solution.py:352
  9.0 1.0 %copy-start = (f32[24,24,24]{2,1,0:T(8,128)S(1)}, f32[24,24,24]{2,1,0:T(8,128)}, u32[]{:S(2)}) copy-start(f32[24,24,24]{2,1,0:T(8,128)} %template_ref.1) | copy-start | bytes 165892
  10.0 0.8 copy-start.1
  54.0 12.6 %collective-permute-start = (f32[16,120,128]{2,1,0:T(8,128)S(1)}, f32[16,120,128]{2,1,0:T(8,128)S(1)}, u32[]{:S(2)}, u32[]{:S(2)}) collective-permute-start(f32[16,120,128]{2,1,0:T(8,128)S(1)} %all_gather.9.own_ref), channel_id=1, source_target_pairs={{0,8},{8,0},{1,9},{9,1},{2,10},{10,2},{3,11},{11,3},{4,12},{12,4},... | collective-permute-start | bytes 2949128 | tf_op jit(solution)/shard_map/ppermute | solution.py:387

commit v6 on v5

--- a/solution.py
+++ b/solution.py
@@ -257,8 +257,9 @@
     lax.fori_loop(0, 8, expand_first, 0, unroll=2)
 
     def build(i, slot):
-        for tap in range(-1, 4):
+        for tap in range(-1, 4 if i < 6 else 1):
             targets = [(tap, 0)] * (tap >= 0) + [(tap + 1, 1)] * (tap < 3)
+            targets = [(t, p) for t, p in targets if i < 6 or t == 0]
             for four in range(rots // 4):
                 for quad in range(6):
                     moved = []
@@ -276,24 +277,37 @@
                         w8_ref[slot, at, 2 * cell16 : 2 * cell16 + window] = full
                         w8_ref[slot, at, 2 * cell16 + window : 2 * cell16 + 2 * window] = low
 
-    def product(i, slot):
-        here = slice(2 * i * blocks, (2 * i + 16) * blocks)
-        left = jnp.concatenate([l_ref[here, : 24 * window], l_ref[here, 16 * window :]], axis=0)
-        acc_ref[...] += lax.dot_general(left, w_ref[slot], nt, preferred_element_type=f32)
-        left = jnp.concatenate([l8_ref[here, : 48 * window], l8_ref[here, 32 * window :]], axis=0)
-        acc8_ref[...] += lax.dot_general(left, w8_ref[slot], nt, preferred_element_type=f32)
+    def product(steps):
+        for left_ref, right_ref, sum_ref, wide in (
+            (l_ref, w_ref, acc_ref, window),
+            (l8_ref, w8_ref, acc8_ref, 2 * window),
+        ):
+            left, right = ([], []), []
+            for i in steps:
+                here = slice(2 * i * blocks, (2 * i + 16) * blocks)
+                pieces = [(0, 24 * wide)] if i < 6 else [(4 * quad * wide, wide) for quad in range(6)]
+                for start, size in pieces:
+                    for plane in range(2):
+                        at = start + 16 * plane * wide
+                        left[plane].append(left_ref[here, at : at + size])
+                    right.append(right_ref[i % 4, :, start : start + size])
+            both = jnp.concatenate([jnp.concatenate(part, axis=1) for part in left], axis=0)
+            sum_ref[...] += lax.dot_general(
+                both, jnp.concatenate(right, axis=1), nt, preferred_element_type=f32
+            )
 
     acc_ref[...] = jnp.zeros_like(acc_ref)
     acc8_ref[...] = jnp.zeros_like(acc8_ref)
     build(0, 0)
-    for i in range(7):
-        if i < 2:
-            for r in range(8 * i, 8 * i + 8):
+    groups = (0,), (1, 2), (3, 4), (5, 6)
+    for k, group in enumerate(groups):
+        if k == 1:
+            for r in range(rots):
                 widen(1, r)
-        if i < 6:
-            build(i + 1, (i + 1) % 2)
-            expand(8 + i)
-        product(i, i % 2)
+        for i in groups[k + 1] if k < 3 else ():
+            build(i, i % 4)
+            expand(i + 7)
+        product(group)
 
     lanes = lax.broadcasted_iota(jnp.int32, (16, window), 1)
     for p in range(2):
@@ -331,8 +345,8 @@
         pltpu.VMEM((rots, 6, 32, window), f32),
         pltpu.VMEM((28 * blocks, 40 * window), bf16),
         pltpu.VMEM((28 * blocks, 80 * window), f8),
-        pltpu.VMEM((2, 256, 24 * window), bf16),
-        pltpu.VMEM((2, 256, 48 * window), f8),
+        pltpu.VMEM((4, 256, 24 * window), bf16),
+        pltpu.VMEM((4, 256, 48 * window), f8),
         pltpu.VMEM((32 * blocks, 256), f32),
         pltpu.VMEM((32 * blocks, 256), f32),
         pltpu.VMEM((32 * blocks, 128), f32),
@@ -392,7 +406,7 @@
         in_specs=[smem, vmem, vmem],
         out_specs=[vmem] * 3,
         scratch_shapes=match_scratch(),
-        compiler_params=pltpu.CompilerParams(vmem_limit_bytes=32 * 2**20),
+        compiler_params=pltpu.CompilerParams(vmem_limit_bytes=44 * 2**20),
         name="match",
     )(place, gathered, partner)
     both = lax.all_gather(theirs, "ylo")

time: 87.4 us -> 86 us (0.984)
  Pallas kernels: 20.7 us -> 19.3 us
    pallas_call x1, Pallas kernels: 16.6 us -> 15.2 us  [shards(): pl.pallas_call(match_kernel, out_shape=[jax.ShapeDtypeStruct((rows, cols)...]
where the time goes in v6:
time: 86 us; the launch traced here: 85.7 us
  blocking collectives  38.5 us (45%)
  Pallas kernels  19.3 us (22%)
  starting transfers between devices  18.2 us (21%)
  waiting for transfers between devices  5.75 us (7%)
  local copies, waits for them, and re-layouts  3.21 us (4%)
    all_gather x1, blocking collectives, shards(): gathered = lax.all_gather(shard, 'z', axis=0, tiled=True)  35.2 us
    pallas_call x1, Pallas kernels, shards(): pl.pallas_call(match_kernel, out_shape=[jax.ShapeDtypeStruct((rows, cols)...  15.2 us
    ppermute x1, starting transfers between devices, shards(): partner = lax.ppermute(gathered, 'core', [(0, 1), (1, 0)])  10.6 us
    all_to_all x1, starting transfers between devices, shards(): lax.all_to_all(copies, group, split_axis=0, concat_axis=0, tiled=True)  7.58 us
    all_to_all x1, waiting for transfers between devices, shards(): lax.all_to_all(copies, group, split_axis=0, concat_axis=0, tiled=True)  3.85 us
    all_gather x1, blocking collectives, shards(): both = lax.all_gather(theirs, 'ylo')  3.27 us
    pallas_call x1, Pallas kernels, shards(): pl.pallas_call(whiten_kernel, out_shape=jax.ShapeDtypeStruct((1, shard_ro...  2.06 us
    pallas_call x1, Pallas kernels, shards(): pl.pallas_call(rotate_kernel, out_shape=[jax.ShapeDtypeStruct((half_rows,...  2.02 us
  transfers between devices with their start and end apart: 2, of which 2 were waited for; matrix products, arithmetic and copies ran while one was open for 0% of the time, Pallas kernels for 2%

profile of v6, /device:TPU:1, one launch (start us, length us, event | category | flops | bytes accessed | tf_op | source)
XLA Modules:
  0.0 85.7 jit_solution(66643824038568996)
XLA Ops:
  0.0 1.4 %broadcast_in_dim.16 = f32[16,32,104]{2,1,0:T(8,128)} broadcast(f32[32,104]{1,0:T(8,128)} %bitcast.15), dimensions={1,2} | broadcast | bytes 226304 | tf_op jit(solution)/shard_map/broadcast_in_dim | solution.py:365
  1.4 7.6 %all-to-all-start = ((f32[16,32,104]{2,1,0:T(8,128)}), f32[16,32,104]{2,1,0:T(8,128)S(1)}, u32[]{:S(2)}, u32[]{:S(2)}) async-start(f32[16,32,104]{2,1,0:T(8,128)} %broadcast_in_dim.16), calls=%async_computation | async-start | bytes 524288 | tf_op jit(solution)/shard_map/all_to_all | solution.py:366
  9.0 0.0 copy-start
  9.1 1.0 %copy-done = f32[24,24,24]{2,1,0:T(8,128)S(1)} copy-done((f32[24,24,24]{2,1,0:T(8,128)S(1)}, f32[24,24,24]{2,1,0:T(8,128)}, u32[]{:S(2)}) %copy-start) | copy-done | bytes 55320
  10.0 0.0 copy-start.1
  10.0 0.8 copy-done.1
  10.8 2.0 %rotate.1 = (f32[56,128]{1,0:T(8,128)S(1)}, bf16[2,864,832]{2,1,0:T(8,128)(2,1)S(1)}) custom-call(s32[1]{0:T(128)} %bitcast.2.core_ref, f32[24,24,24]{2,1,0:T(8,128)S(1)} %copy-done, s32[1,13824]{1,0:T(1,128)S(1)} %copy-done.1, bf16[2,864,832]{2,1,0:T(8,128)(2,1)} %constant.35.clone.f_hbm), custom_call_target="tpu_custom_call" | custom-call | tf_op jit(solution)/shard_map/rotate/pallas_call | solution.py:369
  12.8 3.8 %all-to-all-done.rows_ref = f32[16,32,104]{2,1,0:T(8,128)S(1)} async-done(((f32[16,32,104]{2,1,0:T(8,128)}), f32[16,32,104]{2,1,0:T(8,128)S(1)}, u32[]{:S(2)}, u32[]{:S(2)}) %all-to-all-start) | async-done | bytes 213024 | tf_op jit(solution)/shard_map/all_to_all | solution.py:366
  16.7 2.1 %whiten.1 = f32[1,120,128]{2,1,0:T(8,128)S(1)} custom-call(s32[1]{0:T(128)} %bitcast.3.place_ref, f32[16,32,104]{2,1,0:T(8,128)S(1)} %all-to-all-done.rows_ref, bf16[2,864,832]{2,1,0:T(8,128)(2,1)S(1)} %get-tuple-element.10.f_ref, bf16[2,8,864,128]{3,2,1,0:T(8,128)(2,1)} %constant.36.clone.b_hbm, f32[56,128]{1,0:T(8,128)S(1)} %get-tuple-element.11.own_ref), custom_call_target="tpu_custom_call" | custom-call | tf_op jit(solution)/shard_map/whiten/pallas_call | solution.py:385
  18.8 35.2 %all_gather.9.own_ref = f32[16,120,128]{2,1,0:T(8,128)S(1)} all-gather(f32[1,120,128]{2,1,0:T(8,128)S(1)} %whiten.1), channel_id=1, replica_groups=mesh['ylo'=2,'z'=16,'core'=2,'x'=4,'yhi'=2] {'z'}, dimensions={0}, use_global_device_ids=true | all-gather | bytes 1044480 | tf_op jit(solution)/shard_map/all_gather | solution.py:400
  54.0 10.6 %collective-permute-start = (f32[16,120,128]{2,1,0:T(8,128)S(1)}, f32[16,120,128]{2,1,0:T(8,128)S(1)}, u32[]{:S(2)}, u32[]{:S(2)}) collective-permute-start(f32[16,120,128]{2,1,0:T(8,128)S(1)} %all_gather.9.own_ref), channel_id=1, source_target_pairs={{0,8},{8,0},{1,9},{9,1},{2,10},{10,2},{3,11},{11,3},{4,12},{12,4},... | collective-permute-start | bytes 2949128 | tf_op jit(solution)/shard_map/ppermute | solution.py:401
  64.6 0.1 pad_add_fusion.where_ref
  64.7 1.9 %collective-permute-done.other_ref = f32[16,120,128]{2,1,0:T(8,128)S(1)} collective-permute-done((f32[16,120,128]{2,1,0:T(8,128)S(1)}, f32[16,120,128]{2,1,0:T(8,128)S(1)}, u32[]{:S(2)}, u32[]{:S(2)}) %collective-permute-start) | collective-permute-done | bytes 983072 | tf_op jit(solution)/shard_map/ppermute | solution.py:401
  66.6 15.2 %match.1 = (f32[32,104]{1,0:T(8,128)S(1)}, f32[32,104]{1,0:T(8,128)S(1)}, f32[32,104]{1,0:T(8,128)S(1)}) custom-call(s32[3]{0:T(128)S(1)} %pad_add_fusion.where_ref, f32[16,120,128]{2,1,0:T(8,128)S(1)} %all_gather.9.own_ref, f32[16,120,128]{2,1,0:T(8,128)S(1)} %collective-permute-done.other_ref), custom_call_target="tpu_custom_call" | custom-call | tf_op jit(solution)/shard_map/match/pallas_call | solution.py:403
  81.8 3.3 %all-gather = f32[64,104]{1,0:T(8,128)S(1)} all-gather(f32[32,104]{1,0:T(8,128)S(1)} %get-tuple-element.13), channel_id=2, replica_groups=mesh['ylo'=2,'z'=16,'core'=2,'x'=4,'yhi'=2] {'ylo'}, dimensions={0}, use_global_device_ids=true | all-gather | bytes 39936 | tf_op jit(solution)/shard_map/all_gather | solution.py:412
  85.1 0.6 fusion.1
Async XLA Ops:
  1.4 15.3 %all-to-all-start = ((f32[16,32,104]{2,1,0:T(8,128)}), f32[16,32,104]{2,1,0:T(8,128)S(1)}, u32[]{:S(2)}, u32[]{:S(2)}) async-start(f32[16,32,104]{2,1,0:T(8,128)} %broadcast_in_dim.16), calls=%async_computation | async-start | bytes 524288 | tf_op jit(solution)/shard_map/all_to_all | solution.py:366
  9.0 1.0 %copy-start = (f32[24,24,24]{2,1,0:T(8,128)S(1)}, f32[24,24,24]{2,1,0:T(8,128)}, u32[]{:S(2)}) copy-start(f32[24,24,24]{2,1,0:T(8,128)} %template_ref.1) | copy-start | bytes 165892
  10.0 0.8 copy-start.1
  54.0 12.6 %collective-permute-start = (f32[16,120,128]{2,1,0:T(8,128)S(1)}, f32[16,120,128]{2,1,0:T(8,128)S(1)}, u32[]{:S(2)}, u32[]{:S(2)}) collective-permute-start(f32[16,120,128]{2,1,0:T(8,128)S(1)} %all_gather.9.own_ref), channel_id=1, source_target_pairs={{0,8},{8,0},{1,9},{9,1},{2,10},{10,2},{3,11},{11,3},{4,12},{12,4},... | collective-permute-start | bytes 2949128 | tf_op jit(solution)/shard_map/ppermute | solution.py:401

commit v7 on v6

--- a/solution.py
+++ b/solution.py
@@ -196,7 +196,8 @@
     owner = ((lane + 8 * place + 8) & (window - 1)) // 32
     cell = lax.broadcasted_iota(jnp.int32, (half, window), 1)
 
-    t_ref[...] = jnp.zeros_like(t_ref)
+    t_ref[:, :, :8, :] = jnp.zeros((rots, 6, 8, window), f32)
+    t_ref[:, :, 24:, :] = jnp.zeros((rots, 6, 8, window), f32)
 
     def placed(total, source, lane_from, lane_to, width):
         moved = pltpu.roll(source, (lane_to - lane_from) % window, 1)
@@ -215,12 +216,6 @@
                         source = jnp.where(mine, own_ref[r, at, :], other_ref[r, at, :])
                         total = placed(total, source, lane_from, 32 * part + c, width)
                 t_ref[r, quad, put + low : put + high, :] = total
-
-    def widen_first(r, carry):
-        widen(0, r)
-        return carry
-
-    lax.fori_loop(0, rots, widen_first, 0, unroll=4)
 
     def total_of(u, parity, quad):
         total = None
@@ -250,11 +245,13 @@
         for quad in range(span // 4):
             next_ref[parity, quad] = total_of(0, parity, quad)
 
-    def expand_first(i, carry):
+    def prepare(i, carry):
         expand(i)
+        for r in range(2):
+            widen(0, 2 * i + r)
         return carry
 
-    lax.fori_loop(0, 8, expand_first, 0, unroll=2)
+    lax.fori_loop(0, 8, prepare, 0, unroll=2)
 
     def build(i, slot):
         for tap in range(-1, 4 if i < 6 else 1):
@@ -277,7 +274,7 @@
                         w8_ref[slot, at, 2 * cell16 : 2 * cell16 + window] = full
                         w8_ref[slot, at, 2 * cell16 + window : 2 * cell16 + 2 * window] = low
 
-    def product(steps):
+    def add_products(steps):
         for left_ref, right_ref, sum_ref, wide in (
             (l_ref, w_ref, acc_ref, window),
             (l8_ref, w8_ref, acc8_ref, 2 * window),
@@ -292,12 +289,11 @@
                         left[plane].append(left_ref[here, at : at + size])
                     right.append(right_ref[i % 4, :, start : start + size])
             both = jnp.concatenate([jnp.concatenate(part, axis=1) for part in left], axis=0)
-            sum_ref[...] += lax.dot_general(
+            product = lax.dot_general(
                 both, jnp.concatenate(right, axis=1), nt, preferred_element_type=f32
             )
-
-    acc_ref[...] = jnp.zeros_like(acc_ref)
-    acc8_ref[...] = jnp.zeros_like(acc8_ref)
+            sum_ref[...] = product if 0 in steps else sum_ref[...] + product
+
     build(0, 0)
     groups = (0,), (1, 2), (3, 4), (5, 6)
     for k, group in enumerate(groups):
@@ -307,7 +303,7 @@
         for i in groups[k + 1] if k < 3 else ():
             build(i, i % 4)
             expand(i + 7)
-        product(group)
+        add_products(group)
 
     lanes = lax.broadcasted_iota(jnp.int32, (16, window), 1)
     for p in range(2):

time: 86 us -> 85.6 us (level)
  no operation moved by 1% of the time
where the time goes in v7:
time: 85.6 us; the launch traced here: 85.2 us
  blocking collectives  38.5 us (45%)
  Pallas kernels  18.8 us (22%)
  starting transfers between devices  18.2 us (21%)
  waiting for transfers between devices  5.75 us (7%)
  local copies, waits for them, and re-layouts  3.21 us (4%)
    all_gather x1, blocking collectives, shards(): gathered = lax.all_gather(shard, 'z', axis=0, tiled=True)  35.2 us
    pallas_call x1, Pallas kernels, shards(): pl.pallas_call(match_kernel, out_shape=[jax.ShapeDtypeStruct((rows, cols)...  14.7 us
    ppermute x1, starting transfers between devices, shards(): partner = lax.ppermute(gathered, 'core', [(0, 1), (1, 0)])  10.6 us
    all_to_all x1, starting transfers between devices, shards(): lax.all_to_all(copies, group, split_axis=0, concat_axis=0, tiled=True)  7.58 us
    all_to_all x1, waiting for transfers between devices, shards(): lax.all_to_all(copies, group, split_axis=0, concat_axis=0, tiled=True)  3.85 us
    all_gather x1, blocking collectives, shards(): both = lax.all_gather(theirs, 'ylo')  3.27 us
    pallas_call x1, Pallas kernels, shards(): pl.pallas_call(whiten_kernel, out_shape=jax.ShapeDtypeStruct((1, shard_ro...  2.06 us
    pallas_call x1, Pallas kernels, shards(): pl.pallas_call(rotate_kernel, out_shape=[jax.ShapeDtypeStruct((half_rows,...  2.02 us
  transfers between devices with their start and end apart: 2, of which 2 were waited for; matrix products, arithmetic and copies ran while one was open for 0% of the time, Pallas kernels for 2%

profile of v7, /device:TPU:1, one launch (start us, length us, event | category | flops | bytes accessed | tf_op | source)
XLA Modules:
  0.0 85.2 jit_solution(4869704267228573435)
XLA Ops:
  0.0 1.4 %broadcast_in_dim.16 = f32[16,32,104]{2,1,0:T(8,128)} broadcast(f32[32,104]{1,0:T(8,128)} %bitcast.15), dimensions={1,2} | broadcast | bytes 226304 | tf_op jit(solution)/shard_map/broadcast_in_dim | solution.py:361
  1.4 7.6 %all-to-all-start = ((f32[16,32,104]{2,1,0:T(8,128)}), f32[16,32,104]{2,1,0:T(8,128)S(1)}, u32[]{:S(2)}, u32[]{:S(2)}) async-start(f32[16,32,104]{2,1,0:T(8,128)} %broadcast_in_dim.16), calls=%async_computation | async-start | bytes 524288 | tf_op jit(solution)/shard_map/all_to_all | solution.py:362
  9.0 0.0 copy-start
  9.1 1.0 %copy-done = f32[24,24,24]{2,1,0:T(8,128)S(1)} copy-done((f32[24,24,24]{2,1,0:T(8,128)S(1)}, f32[24,24,24]{2,1,0:T(8,128)}, u32[]{:S(2)}) %copy-start) | copy-done | bytes 55320
  10.0 0.0 copy-start.1
  10.0 0.8 copy-done.1
  10.8 2.0 %rotate.1 = (f32[56,128]{1,0:T(8,128)S(1)}, bf16[2,864,832]{2,1,0:T(8,128)(2,1)S(1)}) custom-call(s32[1]{0:T(128)} %bitcast.2.core_ref, f32[24,24,24]{2,1,0:T(8,128)S(1)} %copy-done, s32[1,13824]{1,0:T(1,128)S(1)} %copy-done.1, bf16[2,864,832]{2,1,0:T(8,128)(2,1)} %constant.35.clone.f_hbm), custom_call_target="tpu_custom_call" | custom-call | tf_op jit(solution)/shard_map/rotate/pallas_call | solution.py:365
  12.8 3.8 %all-to-all-done.rows_ref = f32[16,32,104]{2,1,0:T(8,128)S(1)} async-done(((f32[16,32,104]{2,1,0:T(8,128)}), f32[16,32,104]{2,1,0:T(8,128)S(1)}, u32[]{:S(2)}, u32[]{:S(2)}) %all-to-all-start) | async-done | bytes 213024 | tf_op jit(solution)/shard_map/all_to_all | solution.py:362
  16.7 2.1 %whiten.1 = f32[1,120,128]{2,1,0:T(8,128)S(1)} custom-call(s32[1]{0:T(128)} %bitcast.3.place_ref, f32[16,32,104]{2,1,0:T(8,128)S(1)} %all-to-all-done.rows_ref, bf16[2,864,832]{2,1,0:T(8,128)(2,1)S(1)} %get-tuple-element.10.f_ref, bf16[2,8,864,128]{3,2,1,0:T(8,128)(2,1)} %constant.36.clone.b_hbm, f32[56,128]{1,0:T(8,128)S(1)} %get-tuple-element.11.own_ref), custom_call_target="tpu_custom_call" | custom-call | tf_op jit(solution)/shard_map/whiten/pallas_call | solution.py:381
  18.8 35.2 %all_gather.9.own_ref = f32[16,120,128]{2,1,0:T(8,128)S(1)} all-gather(f32[1,120,128]{2,1,0:T(8,128)S(1)} %whiten.1), channel_id=1, replica_groups=mesh['ylo'=2,'z'=16,'core'=2,'x'=4,'yhi'=2] {'z'}, dimensions={0}, use_global_device_ids=true | all-gather | bytes 1044480 | tf_op jit(solution)/shard_map/all_gather | solution.py:396
  54.0 10.6 %collective-permute-start = (f32[16,120,128]{2,1,0:T(8,128)S(1)}, f32[16,120,128]{2,1,0:T(8,128)S(1)}, u32[]{:S(2)}, u32[]{:S(2)}) collective-permute-start(f32[16,120,128]{2,1,0:T(8,128)S(1)} %all_gather.9.own_ref), channel_id=1, source_target_pairs={{0,8},{8,0},{1,9},{9,1},{2,10},{10,2},{3,11},{11,3},{4,12},{12,4},... | collective-permute-start | bytes 2949128 | tf_op jit(solution)/shard_map/ppermute | solution.py:397
  64.6 0.1 pad_add_fusion.where_ref
  64.7 1.9 %collective-permute-done.other_ref = f32[16,120,128]{2,1,0:T(8,128)S(1)} collective-permute-done((f32[16,120,128]{2,1,0:T(8,128)S(1)}, f32[16,120,128]{2,1,0:T(8,128)S(1)}, u32[]{:S(2)}, u32[]{:S(2)}) %collective-permute-start) | collective-permute-done | bytes 983072 | tf_op jit(solution)/shard_map/ppermute | solution.py:397
  66.6 14.7 %match.1 = (f32[32,104]{1,0:T(8,128)S(1)}, f32[32,104]{1,0:T(8,128)S(1)}, f32[32,104]{1,0:T(8,128)S(1)}) custom-call(s32[3]{0:T(128)S(1)} %pad_add_fusion.where_ref, f32[16,120,128]{2,1,0:T(8,128)S(1)} %all_gather.9.own_ref, f32[16,120,128]{2,1,0:T(8,128)S(1)} %collective-permute-done.other_ref), custom_call_target="tpu_custom_call" | custom-call | tf_op jit(solution)/shard_map/match/pallas_call | solution.py:399
  81.3 3.3 %all-gather = f32[64,104]{1,0:T(8,128)S(1)} all-gather(f32[32,104]{1,0:T(8,128)S(1)} %get-tuple-element.13), channel_id=2, replica_groups=mesh['ylo'=2,'z'=16,'core'=2,'x'=4,'yhi'=2] {'ylo'}, dimensions={0}, use_global_device_ids=true | all-gather | bytes 39936 | tf_op jit(solution)/shard_map/all_gather | solution.py:408
  84.6 0.6 fusion.1
Async XLA Ops:
  1.4 15.3 %all-to-all-start = ((f32[16,32,104]{2,1,0:T(8,128)}), f32[16,32,104]{2,1,0:T(8,128)S(1)}, u32[]{:S(2)}, u32[]{:S(2)}) async-start(f32[16,32,104]{2,1,0:T(8,128)} %broadcast_in_dim.16), calls=%async_computation | async-start | bytes 524288 | tf_op jit(solution)/shard_map/all_to_all | solution.py:362
  9.0 1.0 %copy-start = (f32[24,24,24]{2,1,0:T(8,128)S(1)}, f32[24,24,24]{2,1,0:T(8,128)}, u32[]{:S(2)}) copy-start(f32[24,24,24]{2,1,0:T(8,128)} %template_ref.1) | copy-start | bytes 165892
  10.0 0.8 copy-start.1
  54.0 12.6 %collective-permute-start = (f32[16,120,128]{2,1,0:T(8,128)S(1)}, f32[16,120,128]{2,1,0:T(8,128)S(1)}, u32[]{:S(2)}, u32[]{:S(2)}) collective-permute-start(f32[16,120,128]{2,1,0:T(8,128)S(1)} %all_gather.9.own_ref), channel_id=1, source_target_pairs={{0,8},{8,0},{1,9},{9,1},{2,10},{10,2},{3,11},{11,3},{4,12},{12,4},... | collective-permute-start | bytes 2949128 | tf_op jit(solution)/shard_map/ppermute | solution.py:397

commit v8 on v7

--- a/solution.py
+++ b/solution.py
@@ -311,7 +311,7 @@
         best = acc_ref[:, at] + acc8_ref[:, at] * (1.0 / (volume_low * template_full))
         for shift in (64, 32, 16, 8):
             best = jnp.maximum(best, pltpu.roll(best, shift, 1))
-        best_ref[...] = best
+        best_ref[: 32 * blocks, :] = best
         for plane in range(2):
             score = jnp.zeros((16, window), f32)
             for block in range(13):
@@ -345,8 +345,8 @@
         pltpu.VMEM((4, 256, 48 * window), f8),
         pltpu.VMEM((32 * blocks, 256), f32),
         pltpu.VMEM((32 * blocks, 256), f32),
-        pltpu.VMEM((32 * blocks, 128), f32),
-        pltpu.VMEM((2 * rows, 128), f32),
+        pltpu.VMEM((33 * blocks, 128), f32),
+        pltpu.VMEM((2 * rows + 8, 128), f32),
         pltpu.VMEM((2, span // 4, blocks, window), f32),
     ]
 

time: 85.6 us -> 85.6 us (level)
  no operation moved by 1% of the time
where the time goes in v8:
time: 85.6 us; the launch traced here: 85.2 us
  blocking collectives  38.5 us (45%)
  Pallas kernels  18.8 us (22%)
  starting transfers between devices  18.2 us (21%)
  waiting for transfers between devices  5.75 us (7%)
  local copies, waits for them, and re-layouts  3.21 us (4%)
    all_gather x1, blocking collectives, shards(): gathered = lax.all_gather(shard, 'z', axis=0, tiled=True)  35.2 us
    pallas_call x1, Pallas kernels, shards(): pl.pallas_call(match_kernel, out_shape=[jax.ShapeDtypeStruct((rows, cols)...  14.7 us
    ppermute x1, starting transfers between devices, shards(): partner = lax.ppermute(gathered, 'core', [(0, 1), (1, 0)])  10.6 us
    all_to_all x1, starting transfers between devices, shards(): lax.all_to_all(copies, group, split_axis=0, concat_axis=0, tiled=True)  7.58 us
    all_to_all x1, waiting for transfers between devices, shards(): lax.all_to_all(copies, group, split_axis=0, concat_axis=0, tiled=True)  3.85 us
    all_gather x1, blocking collectives, shards(): both = lax.all_gather(theirs, 'ylo')  3.27 us
    pallas_call x1, Pallas kernels, shards(): pl.pallas_call(whiten_kernel, out_shape=jax.ShapeDtypeStruct((1, shard_ro...  2.06 us
    pallas_call x1, Pallas kernels, shards(): pl.pallas_call(rotate_kernel, out_shape=[jax.ShapeDtypeStruct((half_rows,...  2.02 us
  transfers between devices with their start and end apart: 2, of which 2 were waited for; matrix products, arithmetic and copies ran while one was open for 0% of the time, Pallas kernels for 2%

profile of v8, /device:TPU:1, one launch (start us, length us, event | category | flops | bytes accessed | tf_op | source)
XLA Modules:
  0.0 85.2 jit_solution(10525693681707947496)
XLA Ops:
  0.0 1.4 %broadcast_in_dim.16 = f32[16,32,104]{2,1,0:T(8,128)} broadcast(f32[32,104]{1,0:T(8,128)} %bitcast.15), dimensions={1,2} | broadcast | bytes 226304 | tf_op jit(solution)/shard_map/broadcast_in_dim | solution.py:361
  1.4 7.6 %all-to-all-start = ((f32[16,32,104]{2,1,0:T(8,128)}), f32[16,32,104]{2,1,0:T(8,128)S(1)}, u32[]{:S(2)}, u32[]{:S(2)}) async-start(f32[16,32,104]{2,1,0:T(8,128)} %broadcast_in_dim.16), calls=%async_computation | async-start | bytes 524288 | tf_op jit(solution)/shard_map/all_to_all | solution.py:362
  9.0 0.0 copy-start
  9.1 1.0 %copy-done = f32[24,24,24]{2,1,0:T(8,128)S(1)} copy-done((f32[24,24,24]{2,1,0:T(8,128)S(1)}, f32[24,24,24]{2,1,0:T(8,128)}, u32[]{:S(2)}) %copy-start) | copy-done | bytes 55320
  10.0 0.0 copy-start.1
  10.0 0.8 copy-done.1
  10.8 2.0 %rotate.1 = (f32[56,128]{1,0:T(8,128)S(1)}, bf16[2,864,832]{2,1,0:T(8,128)(2,1)S(1)}) custom-call(s32[1]{0:T(128)} %bitcast.2.core_ref, f32[24,24,24]{2,1,0:T(8,128)S(1)} %copy-done, s32[1,13824]{1,0:T(1,128)S(1)} %copy-done.1, bf16[2,864,832]{2,1,0:T(8,128)(2,1)} %constant.35.clone.f_hbm), custom_call_target="tpu_custom_call" | custom-call | tf_op jit(solution)/shard_map/rotate/pallas_call | solution.py:365
  12.8 3.8 %all-to-all-done.rows_ref = f32[16,32,104]{2,1,0:T(8,128)S(1)} async-done(((f32[16,32,104]{2,1,0:T(8,128)}), f32[16,32,104]{2,1,0:T(8,128)S(1)}, u32[]{:S(2)}, u32[]{:S(2)}) %all-to-all-start) | async-done | bytes 213024 | tf_op jit(solution)/shard_map/all_to_all | solution.py:362
  16.7 2.1 %whiten.1 = f32[1,120,128]{2,1,0:T(8,128)S(1)} custom-call(s32[1]{0:T(128)} %bitcast.3.place_ref, f32[16,32,104]{2,1,0:T(8,128)S(1)} %all-to-all-done.rows_ref, bf16[2,864,832]{2,1,0:T(8,128)(2,1)S(1)} %get-tuple-element.10.f_ref, bf16[2,8,864,128]{3,2,1,0:T(8,128)(2,1)} %constant.36.clone.b_hbm, f32[56,128]{1,0:T(8,128)S(1)} %get-tuple-element.11.own_ref), custom_call_target="tpu_custom_call" | custom-call | tf_op jit(solution)/shard_map/whiten/pallas_call | solution.py:381
  18.8 35.2 %all_gather.9.own_ref = f32[16,120,128]{2,1,0:T(8,128)S(1)} all-gather(f32[1,120,128]{2,1,0:T(8,128)S(1)} %whiten.1), channel_id=1, replica_groups=mesh['ylo'=2,'z'=16,'core'=2,'x'=4,'yhi'=2] {'z'}, dimensions={0}, use_global_device_ids=true | all-gather | bytes 1044480 | tf_op jit(solution)/shard_map/all_gather | solution.py:396
  54.0 10.6 %collective-permute-start = (f32[16,120,128]{2,1,0:T(8,128)S(1)}, f32[16,120,128]{2,1,0:T(8,128)S(1)}, u32[]{:S(2)}, u32[]{:S(2)}) collective-permute-start(f32[16,120,128]{2,1,0:T(8,128)S(1)} %all_gather.9.own_ref), channel_id=1, source_target_pairs={{0,8},{8,0},{1,9},{9,1},{2,10},{10,2},{3,11},{11,3},{4,12},{12,4},... | collective-permute-start | bytes 2949128 | tf_op jit(solution)/shard_map/ppermute | solution.py:397
  64.6 0.1 pad_add_fusion.where_ref
  64.7 1.9 %collective-permute-done.other_ref = f32[16,120,128]{2,1,0:T(8,128)S(1)} collective-permute-done((f32[16,120,128]{2,1,0:T(8,128)S(1)}, f32[16,120,128]{2,1,0:T(8,128)S(1)}, u32[]{:S(2)}, u32[]{:S(2)}) %collective-permute-start) | collective-permute-done | bytes 983072 | tf_op jit(solution)/shard_map/ppermute | solution.py:397
  66.6 14.7 %match.1 = (f32[32,104]{1,0:T(8,128)S(1)}, f32[32,104]{1,0:T(8,128)S(1)}, f32[32,104]{1,0:T(8,128)S(1)}) custom-call(s32[3]{0:T(128)S(1)} %pad_add_fusion.where_ref, f32[16,120,128]{2,1,0:T(8,128)S(1)} %all_gather.9.own_ref, f32[16,120,128]{2,1,0:T(8,128)S(1)} %collective-permute-done.other_ref), custom_call_target="tpu_custom_call" | custom-call | tf_op jit(solution)/shard_map/match/pallas_call | solution.py:399
  81.3 3.3 %all-gather = f32[64,104]{1,0:T(8,128)S(1)} all-gather(f32[32,104]{1,0:T(8,128)S(1)} %get-tuple-element.13), channel_id=2, replica_groups=mesh['ylo'=2,'z'=16,'core'=2,'x'=4,'yhi'=2] {'ylo'}, dimensions={0}, use_global_device_ids=true | all-gather | bytes 39936 | tf_op jit(solution)/shard_map/all_gather | solution.py:408
  84.6 0.6 fusion.1
Async XLA Ops:
  1.4 15.3 %all-to-all-start = ((f32[16,32,104]{2,1,0:T(8,128)}), f32[16,32,104]{2,1,0:T(8,128)S(1)}, u32[]{:S(2)}, u32[]{:S(2)}) async-start(f32[16,32,104]{2,1,0:T(8,128)} %broadcast_in_dim.16), calls=%async_computation | async-start | bytes 524288 | tf_op jit(solution)/shard_map/all_to_all | solution.py:362
  9.0 1.0 %copy-start = (f32[24,24,24]{2,1,0:T(8,128)S(1)}, f32[24,24,24]{2,1,0:T(8,128)}, u32[]{:S(2)}) copy-start(f32[24,24,24]{2,1,0:T(8,128)} %template_ref.1) | copy-start | bytes 165892
  10.0 0.8 copy-start.1
  54.0 12.6 %collective-permute-start = (f32[16,120,128]{2,1,0:T(8,128)S(1)}, f32[16,120,128]{2,1,0:T(8,128)S(1)}, u32[]{:S(2)}, u32[]{:S(2)}) collective-permute-start(f32[16,120,128]{2,1,0:T(8,128)S(1)} %all_gather.9.own_ref), channel_id=1, source_target_pairs={{0,8},{8,0},{1,9},{9,1},{2,10},{10,2},{3,11},{11,3},{4,12},{12,4},... | collective-permute-start | bytes 2949128 | tf_op jit(solution)/shard_map/ppermute | solution.py:397
